TPU v7x, 512 devices: a whole 4x4x16 slice. The times are simulated.
512 devices in a mesh: seq: 64 (over z_lo, x, y), dp: 8 (over z_hi, core).
Axes of the slice: x: 4, y: 4, z: 16 (z_hi: 4, z_lo: 4; z = z_hi * 4 + z_lo), core: 2. Of those that a mesh axis runs over, the one named last changes fastest.
Arguments:
- tokens: bfloat16 [16, 64, 128, 1152], P('dp', 'seq'), may hold values from -6 to 6
- modulation: float32 [16, 3, 1152], P('dp'), may hold values from -2.5 to 2.5
- cotangent: bfloat16 [16, 64, 128, 1152], P('dp', 'seq'), may hold values from -13 to 13
- qkv_weight: bfloat16 [1152, 3456], P('seq', 'dp'), may hold values from -0.1875 to 0.1875
- out_weight: bfloat16 [1152, 1152], P('seq', 'dp'), may hold values from -0.1875 to 0.1875
Outputs:
- grad_tokens: bfloat16 [16, 64, 128, 1152], P('dp', 'seq')
- grad_modulation: float32 [16, 2, 1152], P('dp')
All inputs are finite; a program needn't handle non-finite values.
Results may differ from a plain program's by a relative error of at most 0.0071.
Values may be sent and summed in bfloat16 or wider, within the bound.
A program may use at most 128 MiB of HBM per device.

v0:
```python
import math

import jax
import jax.numpy as jnp
from jax import lax
from jax.sharding import PartitionSpec as P

H = 16


EPS = 1e-06


def project(row_block, matrix):
    lead_shape = row_block.shape[:-1]
    result = jnp.dot(
        row_block.reshape(-1, row_block.shape[-1]), matrix, preferred_element_type=jnp.float32
    )
    return result.reshape(lead_shape + (matrix.shape[1],))


def back_project(row_block, matrix):
    lead_shape = row_block.shape[:-1]
    result = lax.dot_general(
        row_block.reshape(-1, row_block.shape[-1]),
        matrix,
        (((1,), (1,)), ((), ())),
        preferred_element_type=jnp.float32,
    )
    return result.reshape(lead_shape + (matrix.shape[0],))


def attend_back(projected, grad_attn, head_count):
    clip_count, frames, patches, triple = projected.shape
    head_size = triple // (3 * head_count)
    split = projected.reshape(clip_count, frames, patches, 3, head_count, head_size)
    query = split[:, :, :, 0]
    keys = split[:, :, :, 1]
    values = split[:, :, :, 2]
    grad_heads = grad_attn.reshape(clip_count, frames, patches, head_count, head_size)
    score_scale = 1.0 / math.sqrt(head_size)
    scores = (
        jnp.einsum("cfphe,cgphe->cphfg", query, keys, preferred_element_type=jnp.float32)
        * score_scale
    )
    exp_scores = jnp.exp(scores)
    attn_probs = exp_scores / jnp.sum(exp_scores, axis=-1, keepdims=True)
    probs_low = attn_probs.astype(jnp.bfloat16)
    grad_probs = jnp.einsum(
        "cfphe,cgphe->cphfg", grad_heads, values, preferred_element_type=jnp.float32
    )
    inner = jnp.sum(attn_probs * grad_probs, axis=-1, keepdims=True)
    grad_scores = (attn_probs * (grad_probs - inner) * score_scale).astype(jnp.bfloat16)
    grad_query = jnp.einsum(
        "cphfg,cgphe->cfphe", grad_scores, keys, preferred_element_type=jnp.float32
    )
    grad_keys = jnp.einsum(
        "cphfg,cfphe->cgphe", grad_scores, query, preferred_element_type=jnp.float32
    )
    grad_values = jnp.einsum(
        "cphfg,cfphe->cgphe", probs_low, grad_heads, preferred_element_type=jnp.float32
    )
    grad_proj = jnp.stack([grad_query, grad_keys, grad_values], axis=3).astype(jnp.bfloat16)
    return grad_proj.reshape(clip_count, frames, patches, triple)


def norm_forward(tokens, cotangent, modulation):
    tokens_wide = tokens.astype(jnp.float32)
    mean_val = jnp.mean(tokens_wide, axis=-1, keepdims=True)
    centred = tokens_wide - mean_val
    inv_std = lax.rsqrt(jnp.mean(centred * centred, axis=-1, keepdims=True) + EPS)
    normed = centred * inv_std
    mod_shift = modulation[:, 0][:, None, None, :]
    mod_scale = modulation[:, 1][:, None, None, :]
    mod_gate = modulation[:, 2][:, None, None, :]
    hidden = (normed * (1.0 + mod_scale) + mod_shift).astype(jnp.bfloat16)
    gated_grad = (cotangent.astype(jnp.float32) * mod_gate).astype(jnp.bfloat16)
    return (normed, inv_std, hidden, gated_grad)


def norm_backward(grad_hidden, normed, inv_std, cotangent, modulation):
    mod_scale = modulation[:, 1][:, None, None, :]
    local_sums = jnp.stack(
        [jnp.sum(grad_hidden, axis=(1, 2)), jnp.sum(grad_hidden * normed, axis=(1, 2))], axis=1
    )
    grad_normed = grad_hidden * (1.0 + mod_scale)
    mean_grad = jnp.mean(grad_normed, axis=-1, keepdims=True)
    mean_cross = jnp.mean(grad_normed * normed, axis=-1, keepdims=True)
    grad_tokens = cotangent.astype(jnp.float32) + inv_std * (
        grad_normed - mean_grad - normed * mean_cross
    )
    return (grad_tokens.astype(jnp.bfloat16), local_sums)


def local(tokens, modulation, cotangent, qkv_weight, out_weight):
    part_qkv, part_out = (
        lax.all_gather(qkv_weight, "dp", axis=1, tiled=True),
        lax.all_gather(out_weight, "dp", axis=1, tiled=True),
    )
    full_qkv, full_out = (
        lax.all_gather(part_qkv, "seq", axis=0, tiled=True),
        lax.all_gather(part_out, "seq", axis=0, tiled=True),
    )
    normed, inv_std, hidden, gated_grad = norm_forward(tokens, cotangent, modulation)
    projected = project(hidden, full_qkv).astype(jnp.bfloat16)
    projected_t = lax.all_to_all(projected, "seq", split_axis=2, concat_axis=1, tiled=True)
    grad_attn = back_project(gated_grad, full_out).astype(jnp.bfloat16)
    grad_attn_t = lax.all_to_all(grad_attn, "seq", split_axis=2, concat_axis=1, tiled=True)
    grad_proj_t = attend_back(projected_t, grad_attn_t, H)
    grad_proj = lax.all_to_all(grad_proj_t, "seq", split_axis=1, concat_axis=2, tiled=True)
    grad_hidden = back_project(grad_proj, full_qkv)
    grad_tokens, local_sums = norm_backward(grad_hidden, normed, inv_std, cotangent, modulation)
    grad_modulation = lax.psum(local_sums, "seq")
    return (grad_tokens, grad_modulation)


def solution(mesh):
    in_specs = (
        P("dp", "seq", None, None),
        P("dp", None, None),
        P("dp", "seq", None, None),
        P("seq", "dp"),
        P("seq", "dp"),
    )
    out_specs = (P("dp", "seq", None, None), P("dp", None, None))
    return jax.shard_map(local, mesh=mesh, in_specs=in_specs, out_specs=out_specs, check_vma=False)
```

profile of v0, /device:TPU:128, one launch (start us, length us, event | category | flops | bytes accessed | tf_op | source)
XLA Modules:
  0.0 1277.9 jit_solution(7112435510966680652)
XLA Ops:
  7.2 0.0 all-gather.9.cloned.1.call-start
  7.2 22.0 %all-gather.2 = bf16[8,144,18]{1,2,0:T(8,128)(2,1)S(1)} all-gather(bf16[1,144,18]{1,2,0:T(8,128)(2,1)} %bitcast.92), channel_id=1, replica_groups=mesh['seq'=64,'dp'=8] {'dp'}, dimensions={0}, use_global_device_ids=true | all-gather | bytes 46656 | tf_op jit(solution)/shard_map/all_gather | solution.py:98
  29.2 0.8 reshape.136
  30.0 0.0 all-gather.9.cloned.1.call-update
  30.0 0.0 all-gather.7.cloned.1.call-start
  30.1 18.4 %all-gather = bf16[8,432,18]{1,2,0:T(8,128)(2,1)S(1)} all-gather(bf16[1,432,18]{1,2,0:T(8,128)(2,1)} %bitcast.91), channel_id=1, replica_groups=mesh['seq'=64,'dp'=8] {'dp'}, dimensions={0}, use_global_device_ids=true | all-gather | bytes 139968 | tf_op jit(solution)/shard_map/all_gather | solution.py:97
  48.6 0.9 reshape.132
  49.5 0.0 all-gather.7.cloned.1.call-update
  49.5 0.7 add_bitcast_fusion
  50.3 337.5 %all-gather.9.cloned.1.call-done = bf16[64,18,1152]{2,1,0:T(8,128)(2,1)} async-done(((bf16[1,18,1152]{2,1,0:T(8,128)(2,1)}), bf16[64,18,1152]{2,1,0:T(8,128)(2,1)}) %all-gather.9.cloned.1.call-update) | async-done | bytes 2654224 | tf_op jit(solution)/shard_map/all_gather | solution.py:102
  387.8 3.9 reshape.140
  391.7 1.1 fusion.2
  392.8 1.4 copy.57
  394.2 9.3 all-to-all-start.1
  403.5 0.2 convert_reduce_fusion
  403.7 0.3 fusion.39
  404.0 360.0 %all-gather.7.cloned.1.call-done = bf16[64,18,3456]{2,1,0:T(8,128)(2,1)} async-done(((bf16[1,18,3456]{2,1,0:T(8,128)(2,1)}), bf16[64,18,3456]{2,1,0:T(8,128)(2,1)}) %all-gather.7.cloned.1.call-update) | async-done | bytes 7962640 | tf_op jit(solution)/shard_map/all_gather | solution.py:101
  764.0 13.2 %reshape.139 = bf16[1152,3456,1]{1,0,2:T(8,128)(2,1)} reshape(bf16[64,18,3456]{2,1,0:T(8,128)(2,1)} %all-gather.7.cloned.1.call-done) | data formatting | bytes 15925248
  777.2 6.0 fusion.1
  783.2 3.1 copy.52
  786.3 9.4 all-to-all-start
  795.7 3.1 reshape.145
  798.9 22.9 %all-to-all-done = bf16[2,1,128,3456]{3,0,1,2:T(2,128)(2,1)} async-done(((bf16[2,1,128,3456]{3,0,1,2:T(2,128)(2,1)}), bf16[2,1,128,3456]{3,0,1,2:T(2,128)(2,1)}, u32[]{:S(2)}, u32[]{:S(2)}) %all-to-all-start) | async-done | bytes 1769504 | tf_op jit(solution)/shard_map/all_to_all | solution.py:106
  821.8 8.7 reshape.144
  830.5 1.0 fusion.68
  831.5 0.2 copy-done.2
  831.7 2.7 fusion.43
  834.4 1.7 fusion.7
  836.1 1.3 copy-done.7
  837.4 1.1 fusion.26
  838.5 0.1 copy-done.6
  838.6 6.1 fusion.27
  844.7 6.3 fusion.30
  851.0 2.0 pad_maximum_fusion
  853.0 2.0 copy.70
  855.0 6.9 reshape.143
  861.9 5.1 all-to-all-start.2
  867.1 13.2 %reshape.134 = bf16[1152,3456]{1,0:T(8,128)(2,1)} reshape(bf16[64,18,3456]{2,1,0:T(8,128)(2,1)} %all-gather.7.cloned.1.call-done) | data formatting | bytes 15925248
  880.3 13.1 %all-to-all-done.2 = bf16[2,64,2,3456]{3,2,0,1:T(2,128)(2,1)S(1)} async-done(((bf16[2,64,2,3456]{3,2,0,1:T(2,128)(2,1)}), bf16[2,64,2,3456]{3,2,0,1:T(2,128)(2,1)S(1)}, u32[]{:S(2)}, u32[]{:S(2)}) %all-to-all-start.2) | async-done | bytes 1769504 | tf_op jit(solution)/shard_map/all_to_all | solution.py:110
  893.4 2.4 copy.65
  895.8 4.0 reshape.129
  899.8 6.0 fusion.42
  905.8 0.0 copy-start.10
  905.8 0.5 fusion.38
  906.3 0.1 reduce_sum.78
  906.4 362.7 %psum.7 = f32[2,2,1152]{2,0,1:T(2,128)S(1)} all-reduce(f32[2,2,1152]{2,0,1:T(2,128)S(1)} %pad_maximum_fusion.1), channel_id=1, replica_groups=mesh['seq'=64,'dp'=8] {'seq'}, use_global_device_ids=true, to_apply=%region_8.0 | all-reduce | flops 4608 | bytes 36864 | tf_op jit(solution)/shard_map/psum | solution.py:113
  1269.1 0.6 copy.68
  1269.7 1.3 fusion.41
  (32 shorter events, 0.2 us)
Async XLA Ops:
  7.2 380.7 %all-gather.9.cloned.1.call-start = ((), (), s32[]{:S(2)}) async-start(), calls=%async_computation.4 | async-start | bytes 3594240 | tf_op jit(solution)/shard_map/all_gather | solution.py:102
  30.0 734.0 %all-gather.7.cloned.1.call-start = ((), (), s32[]{:S(2)}) async-start(), calls=%async_computation.3 | async-start | bytes 10782720 | tf_op jit(solution)/shard_map/all_gather | solution.py:101
  50.3 341.4 %copy-start.9 = (bf16[2,1,128,1152]{3,2,1,0:T(8,128)(2,1)S(1)}, bf16[2,1,128,1152]{3,2,1,0:T(8,128)(2,1)}, u32[]{:S(2)}) copy-start(bf16[2,1,128,1152]{3,2,1,0:T(8,128)(2,1)} %param.7) | copy-start | bytes 1769476
  392.8 10.7 copy-start
  394.2 392.1 %all-to-all-start.1 = ((bf16[2,1,128,1152]{3,0,1,2:T(2,128)(2,1)}), bf16[2,1,128,1152]{3,0,1,2:T(2,128)(2,1)S(1)}, u32[]{:S(2)}, u32[]{:S(2)}) async-start(bf16[2,1,128,1152]{3,0,1,2:T(2,128)(2,1)} %copy.57), calls=%async_computation.1 | async-start | bytes 1179648 | tf_op jit(solution)/shard_map/all_to_all | solution.py:108
  404.0 373.2 %copy-start.11 = (f32[2,128]{1,0:T(2,128)}, f32[2,128]{1,0:T(2,128)S(1)}, u32[]{:S(2)}) copy-start(f32[2,128]{1,0:T(2,128)S(1)} %add_rsqrt_fusion) | copy-start | bytes 3076
  786.3 35.5 %all-to-all-start = ((bf16[2,1,128,3456]{3,0,1,2:T(2,128)(2,1)}), bf16[2,1,128,3456]{3,0,1,2:T(2,128)(2,1)}, u32[]{:S(2)}, u32[]{:S(2)}) async-start(bf16[2,1,128,3456]{3,0,1,2:T(2,128)(2,1)} %copy.52), calls=%async_computation | async-start | bytes 3538944 | tf_op jit(solution)/shard_map/all_to_all | solution.py:106
  830.5 1.2 copy-start.2
  831.4 2.9 copy-start.3
  831.5 2.9 copy-start.5
  836.0 1.3 copy-start.7
  837.4 1.2 copy-start.6
  838.6 6.1 copy-start.4
  844.7 6.3 copy-start.8
  861.9 31.5 %all-to-all-start.2 = ((bf16[2,64,2,3456]{3,2,0,1:T(2,128)(2,1)}), bf16[2,64,2,3456]{3,2,0,1:T(2,128)(2,1)S(1)}, u32[]{:S(2)}, u32[]{:S(2)}) async-start(bf16[2,64,2,3456]{3,2,0,1:T(2,128)(2,1)} %reshape.143), calls=%async_computation.2 | async-start | bytes 3538944 | tf_op jit(solution)/shard_map/all_to_all | solution.py:110
  899.8 6.0 copy-start.1
  899.8 6.0 copy-start.12
  905.8 363.9 %copy-start.10 = (bf16[2,1,128,1152]{3,2,1,0:T(8,128)(2,1)S(1)}, bf16[2,1,128,1152]{3,2,1,0:T(8,128)(2,1)}, u32[]{:S(2)}) copy-start(bf16[2,1,128,1152]{3,2,1,0:T(8,128)(2,1)} %param.7) | copy-start | bytes 1769476
  905.8 363.9 %copy-start.13 = (f32[2,128]{1,0:T(2,128)S(1)}, f32[2,128]{1,0:T(2,128)}, u32[]{:S(2)}) copy-start(f32[2,128]{1,0:T(2,128)} %copy-done.11) | copy-start | bytes 3076
Sparse Core Ops, SparseCore 0:
  30.2 357.6 all-gather.8
  389.9 374.0 all-gather.6
where the time goes:
time: 1280 us
  waiting for transfers between devices  734 us (57%)
  blocking collectives  403 us (31%)
  local copies, waits for them, and re-layouts  67 us (5%)
  matrix products  30.9 us (2%)
  starting transfers between devices  23.9 us (2%)
  between operations  14.3 us (1%)
    psum x1, blocking collectives, local(): grad_modulation = lax.psum(local_sums, 'seq')  363 us
    all_gather x1, waiting for transfers between devices, local(): lax.all_gather(part_qkv, 'seq', axis=0, tiled=True)  360 us
    all_gather x1, waiting for transfers between devices, local(): lax.all_gather(part_out, 'seq', axis=0, tiled=True)  338 us
    unnamed x34, local copies, waits for them, and re-layouts  34.3 us
  transfers between devices with their start and end apart: 5, of which 4 were waited for; matrix products, arithmetic and copies ran while one was open for 4% of the time, Pallas kernels for 0%

commit v1 on v0

v1 whole, which is shorter than its diff:
```python
import functools
import math

import jax
import jax.numpy as jnp
import numpy as np
from jax import lax
from jax.experimental import pallas as pl
from jax.experimental.pallas import tpu as pltpu
from jax.sharding import PartitionSpec as P

D = 1152
H = 16
HD = 72
EPS = 1e-06
MESH = pl.DeviceIdType.MESH
BF = jnp.bfloat16
F32 = jnp.float32
RHS_T = (((1,), (1,)), ((), ()))
LHS_T = (((0,), (0,)), ((), ()))


def place_tables():
    tables = np.zeros((2, D, D), np.float32)
    feature = np.arange(D)
    zl, rest = feature // 288, feature % 288
    x, rest = rest // 72, rest % 72
    y, i = rest // 18, rest % 18
    tables[0, feature, y * 288 + x * 72 + zl * 18 + i] = 1
    tables[1, feature, x * 288 + y * 72 + zl * 18 + i] = 1
    return tables


def dot(a, b, dims=(((1,), (0,)), ((), ()))):
    return lax.dot_general(a, b, dims, preferred_element_type=F32)


def iota(shape, dim):
    return lax.broadcasted_iota(jnp.int32, shape, dim)


def pick(source_row, n=256, m=256):
    return (source_row(iota((n, m), 0)) == iota((n, m), 1)).astype(F32).astype(BF)


def kernel(
    tok_ref, mod_ref, cot_ref, wq_ref, wo_ref, table_hbm,
    out_ref, outm_ref,
    sa, ra, sb, rb, z, h, g1, w, table, hid, gated, normed, inv, pr, acc, gp, rr, rr2, ms, mr, ms2, mr2,
    table_sem, zh_s, zh_r, zl_s, zl_r, zc_s, zc_r, p1_s, p1_r, p2_s, p2_r, pc_s, pc_r,
    a_s, a_r, b_s, b_r, c_s, c_r, e_s, e_r, cm_s, cm_r, em_s, em_r,
):
    s, q = lax.axis_index("seq"), lax.axis_index("dp")
    y, x, zl = lax.rem(s, 4), lax.rem(s // 4, 4), s // 16
    zh, c = q // 2, lax.rem(q, 2)
    xy = x * 4 + y
    zfull = zh * 4 + zl
    m4 = lambda v: lax.rem(v + 8, 4)

    def dev(x_, y_, z_, c_):
        return ((lax.rem(z_, 4) * 4 + x_) * 4 + y_, (z_ // 4) * 2 + c_)

    def at_xy(k):
        return dev(m4(x + k // 4), m4(y + lax.rem(k, 4)), zfull, c)

    def at_zl(k):
        return dev(x, y, zh * 4 + m4(zl + k), c)

    def at_zh(k):
        return dev(x, y, m4(zh + k) * 4 + zl, c)

    def at_ring(k):
        return dev(x, y, lax.rem(zfull + k + 16, 16), c)

    other = dev(x, y, zfull, 1 - c)

    def copy(src, dst, ss, rs, to):
        return pltpu.make_async_remote_copy(
            src_ref=src, dst_ref=dst, send_sem=ss, recv_sem=rs, device_id=to, device_id_type=MESH
        )

    tables_in = pltpu.make_async_copy(table_hbm, table, table_sem)
    tables_in.start()

    wide = jnp.concatenate(
        [wq_ref[...].astype(F32), wo_ref[...].astype(F32), jnp.zeros((18, 64), F32)], axis=1
    )
    z[c, zl, zh] = jnp.concatenate([wide, jnp.zeros((14, 640), F32)], axis=0).astype(BF)

    barrier = pltpu.get_barrier_semaphore()

    def greet(to):
        pl.semaphore_signal(barrier, inc=1, device_id=to, device_id_type=MESH)

    greet(other)
    for k in (1, 2, 3):
        greet(at_zh(k))
        greet(at_zl(k))
    for k in (1, -1, 2, -2):
        greet(at_ring(k))

    @pl.loop(1, 16)
    def _(k):
        greet(at_xy(k))

    pl.semaphore_wait(barrier, 26)

    zh_copies = [copy(z.at[c, zl, zh], z.at[c, zl, zh], zh_s.at[k], zh_r.at[k], at_zh(k)) for k in (1, 2, 3)]
    zh_copies = dict(zip((1, 2, 3), zh_copies))
    for k in (1, 2, 3):
        zh_copies[k].start()

    def a_copy(n, k):
        return copy(sa.at[n, lax.rem(x + k // 4, 4) * 4 + lax.rem(y + lax.rem(k, 4), 4)], ra.at[n, xy],
                    a_s.at[n, k], a_r.at[n, k], at_xy(k))

    to_plane = pick(lambda o: ((o >> 3) & 1) * 128 + (o >> 4) * 8 + (o & 7))
    for n, source in enumerate((tok_ref, cot_ref)):
        rows = source[...].reshape(256, D)
        sa[n] = dot(to_plane, rows).astype(BF).reshape(16, 16, D)

        @pl.loop(1, 16)
        def _(k, n=n):
            a_copy(n, k).start()

        ra[n, xy] = sa[n, xy]

    for k in (1, 2, 3):
        zh_copies[k].wait()

    zl_copies = [copy(z.at[c, zl], z.at[c, zl], zl_s.at[n], zl_r.at[n], at_ring(k)) for n, k in enumerate((1, -1, 2))]
    for cp in zl_copies:
        cp.start()

    def b_copy(n, k):
        return copy(sb.at[n, m4(zl + k)], rb.at[n, zl], b_s.at[n, k], b_r.at[n, k], at_zl(k))

    to_line = pick(lambda o: ((o >> 2) & 15) * 16 + ((o >> 1) & 1) * 8 + (o >> 6) * 2 + (o & 1))

    def second_step(n):
        @pl.loop(1, 16)
        def _(k):
            a_copy(n, k).wait()

        sb[n] = dot(to_line, ra[n].reshape(256, D)).astype(BF).reshape(4, 64, D)
        for k in (1, 2, 3):
            b_copy(n, k).start()
        rb[n, zl] = sb[n, zl]

    for cp in zl_copies:
        cp.wait()
    zc = copy(z.at[c], z.at[c], zc_s, zc_r, other)
    zc.start()
    second_step(0)
    zc.wait()

    def block(d):
        return jnp.concatenate([z[d % 2, k, d // 2][0:18, :].astype(F32) for k in range(4)], axis=0)

    blocks = [block(d) for d in range(8)]
    full = jnp.concatenate([b[:, :432] for b in blocks] + [b[:, 432:576] for b in blocks], axis=1)
    full = jnp.concatenate([full, jnp.zeros((8, 4 * D), F32)], axis=0).astype(BF)
    for k in range(4):
        h[k] = full[:, k * D:(k + 1) * D]

    p1_copies = []
    for k in (1, 2, 3):
        p1_copies.append(copy(h.at[2 * c], g1.at[0, x], p1_s.at[0, k], p1_r.at[0, k], dev(m4(x + k), y, zfull, c)))
        p1_copies.append(copy(h.at[2 * c + 1], g1.at[1, y], p1_s.at[1, k], p1_r.at[1, k], dev(x, m4(y + k), zfull, c)))
    for cp in p1_copies:
        cp.start()
    g1[0, x] = h[2 * c]
    g1[1, y] = h[2 * c + 1]

    second_step(1)
    for cp in p1_copies:
        cp.wait()

    squeeze = pick(
        lambda o: o + 8 * ((o >= 72).astype(jnp.int32) + (o >= 144).astype(jnp.int32) + (o >= 216).astype(jnp.int32)),
        288, 320,
    )
    own = (y, x)
    halves = (pl.ds(0, 144), pl.ds(144, 144))
    p2, pc = [], []
    for a in range(2):
        quarter = 2 * c + a
        w[quarter, own[a]] = dot(squeeze, g1[a].reshape(320, D)).astype(BF)
        right = dev(x, m4(y + 1), zfull, c) if a == 0 else dev(m4(x + 1), y, zfull, c)
        left = dev(x, m4(y - 1), zfull, c) if a == 0 else dev(m4(x - 1), y, zfull, c)

        def move(n, slot, half, to, a=a, quarter=quarter):
            ref = w.at[quarter, slot, half]
            return copy(ref, ref, p2_s.at[a, n], p2_r.at[a, n], to)

        me, lo, hi = own[a], m4(own[a] - 1), m4(own[a] + 1)
        p2.append([
            move(0, me, halves[0], right), move(1, me, halves[1], left),
            move(2, me, halves[1], right), move(3, me, halves[0], left),
            move(4, lo, halves[0], right), move(5, hi, halves[1], left),
        ])
        for n in range(4):
            p2[a][n].start()

        def across(n, slot, a=a, quarter=quarter):
            ref = w.at[quarter, slot]
            return copy(ref, ref, pc_s.at[a, n], pc_r.at[a, n], other)

        pc.append([across(0, me), across(1, lo), across(2, hi), across(3, m4(me + 2))])
        pc[a][0].start()

    for n in (0, 1):
        for k in (1, 2, 3):
            b_copy(n, k).wait()
    tables_in.wait()

    def clip_of(rows_shape):
        return ((iota(rows_shape, 0) >> 1) & 1) == 1

    def norm_rows(i):
        rows = pl.ds(pl.multiple_of(i * 32, 32), 32)
        tile = rb.at[0, i // 2][pl.ds(pl.multiple_of(lax.rem(i, 2) * 32, 32), 32), :].astype(F32)
        cot = rb.at[1, i // 2][pl.ds(pl.multiple_of(lax.rem(i, 2) * 32, 32), 32), :].astype(F32)
        mean = jnp.sum(tile, axis=1, keepdims=True) * (1.0 / D)
        centred = tile - mean
        inv_std = lax.rsqrt(jnp.sum(centred * centred, axis=1, keepdims=True) * (1.0 / D) + EPS)
        nrm = centred * inv_std
        normed[rows, :] = nrm
        inv[rows, :] = jnp.broadcast_to(inv_std, (32, 128))
        second = clip_of((32, D))
        shift = jnp.where(second, mod_ref[1, 0:1, :], mod_ref[0, 0:1, :])
        scale = jnp.where(second, mod_ref[1, 1:2, :], mod_ref[0, 1:2, :])
        gate = jnp.where(second, mod_ref[1, 2:3, :], mod_ref[0, 2:3, :])
        hid[0, rows, :] = (nrm * (1.0 + scale) + shift).astype(BF)
        gated[rows, :] = (cot * gate).astype(BF)

    pl.loop(0, 8)(norm_rows)
    hidden = hid[0]
    hid[1] = dot(hidden, table[1]).astype(BF)
    hid[0] = dot(hidden, table[0]).astype(BF)

    for a in range(2):
        p2[a][0].wait()
        p2[a][4].start()
        p2[a][1].wait()
        p2[a][5].start()
    for a in range(2):
        p2[a][2].wait()
        pc[a][1].start()
        p2[a][3].wait()
        pc[a][2].start()
    for a in range(2):
        p2[a][4].wait()
        p2[a][5].wait()
        pc[a][3].start()
    for a in range(2):
        for cp in pc[a]:
            cp.wait()

    def project(i):
        quarter = i // 3
        cols = pl.ds(pl.multiple_of(lax.rem(i, 3) * 384, 128), 384)
        pr[quarter, :, cols] = dot(hid[lax.rem(quarter, 2)], w[quarter, :, :, cols].reshape(D, 384)).astype(BF)

    pl.loop(0, 9)(project)
    ga = dot(gated[...], w[3].reshape(D, D), RHS_T).astype(BF)
    pr[3] = dot(ga, table[1], RHS_T).astype(BF)

    acc[...] = jnp.zeros_like(acc)
    score_scale = 1.0 / math.sqrt(HD)
    same = (iota((256, 256), 0) & 3) == (iota((256, 256), 1) & 3)

    def head(i):
        first = jnp.minimum((i * HD) // 128, 7)
        cols = pl.ds(pl.multiple_of(first * 128, 128), 256)
        lane = iota((256, 256), 1) - (i * HD - first * 128)
        inside = (lane >= 0) & (lane < HD)
        zero = jnp.zeros((256, 256), BF)
        query = jnp.where(inside, pr[0, :, cols], zero)
        keys = jnp.where(inside, pr[1, :, cols], zero)
        values = pr[2, :, cols]
        grad = jnp.where(inside, pr[3, :, cols], zero)
        scores = dot(keys, query, RHS_T) * score_scale
        e = jnp.exp(jnp.where(same, scores, -jnp.inf))
        probs = e / jnp.sum(e, axis=0, keepdims=True)
        grad_probs = dot(values, grad, RHS_T)
        inner = jnp.sum(probs * grad_probs, axis=0, keepdims=True)
        grad_scores = (probs * (grad_probs - inner) * score_scale).astype(BF)
        acc[0, :, cols] += dot(grad_scores, keys, LHS_T)
        acc[1, :, cols] += dot(grad_scores, query)
        acc[2, :, cols] += dot(probs.astype(BF), grad)

    pl.loop(0, H)(head)
    for k in range(3):
        gp[k] = acc[k].astype(BF)

    gha = dot(gp[0], w[0].reshape(D, D), RHS_T) + dot(gp[2], w[2].reshape(D, D), RHS_T)
    ghb = dot(gp[1], w[1].reshape(D, D), RHS_T)
    acc[0] = gha
    acc[1] = ghb
    for k in range(2):
        top = acc[k].astype(BF)
        gp[0] = top
        gp[1] = (acc[k] - top.astype(F32)).astype(BF)
        part = dot(gp[0], table[k], RHS_T) + dot(gp[1], table[k], RHS_T)
        if k == 0:
            acc[2] = part
        else:
            acc[2] += part

    ms[...] = jnp.zeros_like(ms)

    def norm_back(i):
        rows = pl.ds(pl.multiple_of(i * 32, 32), 32)
        inside = pl.ds(pl.multiple_of(lax.rem(i, 2) * 32, 32), 32)
        gh = acc[2, rows, :]
        nrm = normed[rows, :]
        second = clip_of((32, D))
        zero = jnp.zeros_like(gh)
        cross = gh * nrm
        ms[0:1, :] += jnp.sum(jnp.where(second, zero, gh), axis=0, keepdims=True)
        ms[1:2, :] += jnp.sum(jnp.where(second, zero, cross), axis=0, keepdims=True)
        ms[2:3, :] += jnp.sum(jnp.where(second, gh, zero), axis=0, keepdims=True)
        ms[3:4, :] += jnp.sum(jnp.where(second, cross, zero), axis=0, keepdims=True)
        gn = gh * (1.0 + jnp.where(second, mod_ref[1, 1:2, :], mod_ref[0, 1:2, :]))
        mean_grad = jnp.sum(gn, axis=1, keepdims=True) * (1.0 / D)
        mean_cross = jnp.sum(gn * nrm, axis=1, keepdims=True) * (1.0 / D)
        cot = rb.at[1, i // 2][inside, :].astype(F32)
        gt = cot + inv[rows, 0:1] * (gn - mean_grad - nrm * mean_cross)
        rr.at[0, i // 2][inside, :] = gt.astype(BF)

    pl.loop(0, 8)(norm_back)

    back = {}
    for k in (1, 2, 3):
        back[k] = copy(rr.at[0, m4(zl + k)], rr.at[1, zl], c_s.at[k], c_r.at[k], at_zl(k))
        back[k].start()
    mod_back = {}
    for k in (1, 2, 3):
        mod_back[k] = copy(ms, mr.at[zl], cm_s.at[k], cm_r.at[k], at_zl(k))
        mod_back[k].start()
    rr[1, zl] = rr[0, zl]
    mr[zl] = ms[...]
    for k in (1, 2, 3):
        mod_back[k].wait()
    ms2[...] = ((mr[0] + mr[1]) + mr[2]) + mr[3]

    def em_copy(k):
        return copy(ms2, mr2.at[xy], em_s.at[k], em_r.at[k], at_xy(k))

    @pl.loop(1, 16)
    def _(k):
        em_copy(k).start()

    mr2[xy] = ms2[...]
    for k in (1, 2, 3):
        back[k].wait()

    from_line = pick(lambda o: ((o >> 1) & 3) * 64 + (o >> 4) * 4 + ((o >> 3) & 1) * 2 + (o & 1))
    rr2[0] = dot(from_line, rr[1].reshape(256, D)).astype(BF).reshape(16, 16, D)

    def e_copy(k):
        return copy(rr2.at[0, lax.rem(x + k // 4, 4) * 4 + lax.rem(y + lax.rem(k, 4), 4)], rr2.at[1, xy],
                    e_s.at[k], e_r.at[k], at_xy(k))

    @pl.loop(1, 16)
    def _(k):
        e_copy(k).start()

    rr2[1, xy] = rr2[0, xy]

    @pl.loop(1, 16)
    def _(k):
        em_copy(k).wait()

    total = mr2[0]
    for k in range(1, 16):
        total = total + mr2[k]
    outm_ref[0] = total[0:2]
    outm_ref[1] = total[2:4]

    @pl.loop(1, 16)
    def _(k):
        e_copy(k).wait()

    from_plane = pick(lambda o: ((o >> 3) & 15) * 16 + (o >> 7) * 8 + (o & 7))
    out_ref[...] = dot(from_plane, rr2[1].reshape(256, D)).astype(BF).reshape(2, 1, 128, D)


def local(tokens, modulation, cotangent, qkv_weight, out_weight):
    tables = jnp.asarray(place_tables(), BF)
    vmem = pl.BlockSpec(memory_space=pltpu.VMEM)
    dma = pltpu.SemaphoreType.DMA
    return pl.pallas_call(
        kernel,
        out_shape=(
            jax.ShapeDtypeStruct((2, 1, 128, D), BF),
            jax.ShapeDtypeStruct((2, 2, D), F32),
        ),
        in_specs=[vmem] * 5 + [pl.BlockSpec(memory_space=pl.ANY)],
        out_specs=(vmem, vmem),
        scratch_shapes=[
            pltpu.VMEM((2, 16, 16, D), BF),
            pltpu.VMEM((2, 16, 16, D), BF),
            pltpu.VMEM((2, 4, 64, D), BF),
            pltpu.VMEM((2, 4, 64, D), BF),
            pltpu.VMEM((2, 4, 4, 32, 640), BF),
            pltpu.VMEM((4, 80, D), BF),
            pltpu.VMEM((2, 4, 80, D), BF),
            pltpu.VMEM((4, 4, 288, D), BF),
            pltpu.VMEM((2, D, D), BF),
            pltpu.VMEM((2, 256, D), BF),
            pltpu.VMEM((256, D), BF),
            pltpu.VMEM((256, D), F32),
            pltpu.VMEM((256, 128), F32),
            pltpu.VMEM((4, 256, D), BF),
            pltpu.VMEM((3, 256, D), F32),
            pltpu.VMEM((3, 256, D), BF),
            pltpu.VMEM((2, 4, 64, D), BF),
            pltpu.VMEM((2, 16, 16, D), BF),
            pltpu.VMEM((8, D), F32),
            pltpu.VMEM((4, 8, D), F32),
            pltpu.VMEM((8, D), F32),
            pltpu.VMEM((16, 8, D), F32),
            dma,
            dma((4,)), dma((4,)), dma((3,)), dma((3,)), dma, dma,
            dma((2, 4)), dma((2, 4)), dma((2, 6)), dma((2, 6)), dma((2, 4)), dma((2, 4)),
            dma((2, 16)), dma((2, 16)), dma((2, 4)), dma((2, 4)),
            dma((4,)), dma((4,)), dma((16,)), dma((16,)),
            dma((4,)), dma((4,)), dma((16,)), dma((16,)),
        ],
        compiler_params=pltpu.CompilerParams(
            collective_id=0, has_side_effects=True, vmem_limit_bytes=60 * 1024 * 1024
        ),
        name="sublayer_backward",
    )(tokens, modulation, cotangent, qkv_weight, out_weight, tables)


def solution(mesh):
    in_specs = (
        P("dp", "seq", None, None),
        P("dp", None, None),
        P("dp", "seq", None, None),
        P("seq", "dp"),
        P("seq", "dp"),
    )
    out_specs = (P("dp", "seq", None, None), P("dp", None, None))
    return jax.shard_map(local, mesh=mesh, in_specs=in_specs, out_specs=out_specs, check_vma=False)
```

time: 1280 us -> 148 us (0.12)
  the two profiles are of different devices: /device:TPU:128 before, /device:TPU:1 now
where the time goes in v1:
time: 148 us
  Pallas kernels  142 us (96%)
  local copies, waits for them, and re-layouts  4.62 us (3%)
    pallas_call x1, Pallas kernels, local(): pl.pallas_call(kernel, out_shape=(jax.ShapeDtypeStruct((2, 1, 128, D), BF...  142 us
    unnamed x3, local copies, waits for them, and re-layouts  4.62 us

profile of v1, /device:TPU:1, one launch (start us, length us, event | category | flops | bytes accessed | tf_op | source)
XLA Modules:
  0.0 147.5 jit_solution(13810891231423356641)
XLA Ops:
  0.6 1.4 copy.8.mod_ref
  2.0 142.2 %sublayer_backward.1 = (bf16[2,1,128,1152]{3,2,1,0:T(8,128)(2,1)}, f32[2,2,1152]{2,1,0:T(2,128)}) custom-call(bf16[2,1,128,1152]{3,2,1,0:T(8,128)(2,1)} %tok_ref.1, f32[2,3,1152]{2,1,0:T(4,128)} %copy.8.mod_ref, bf16[2,1,128,1152]{3,2,1,0:T(8,128)(2,1)} %cot_ref.1, bf16[18,432]{1,0:T(8,128)(2,1)} %wq_ref.1, bf16[18,144]{1,0:T(8,128)(2,1)} %wo_ref.1, ...), custom_call_target="tpu_custom_call" | custom-call | tf_op jit(solution)/shard_map/sublayer_backward/pallas_call | solution.py:394
  144.3 1.9 %copy.11 = bf16[2,1,128,1152]{3,2,1,0:T(8,128)(2,1)} copy(bf16[2,1,128,1152]{3,2,1,0:T(8,128)(2,1)} %get-tuple-element.4) | data formatting | bytes 1179648
  146.2 1.3 copy.12

commit v2 on v1

v2 whole, which is shorter than its diff:
```python
import functools
import math

import jax
import jax.numpy as jnp
import numpy as np
from jax import lax
from jax.experimental import pallas as pl
from jax.experimental.pallas import tpu as pltpu
from jax.sharding import PartitionSpec as P

D = 1152
H = 16
HD = 72
EPS = 1e-06
MESH = pl.DeviceIdType.MESH
BF = jnp.bfloat16
F32 = jnp.float32
RHS_T = (((1,), (1,)), ((), ()))
LHS_T = (((0,), (0,)), ((), ()))


MAIN, TAIL = 1024, 256


def place_table():
    table = np.zeros((D, MAIN + 2 * TAIL), np.float32)
    for feature in range(D):
        zl, rest = divmod(feature, 288)
        position, i = divmod(rest, 18)
        t = zl * 18 + i
        if t < 64:
            table[feature, position * 64 + t] = 1
        else:
            table[feature, MAIN + position * 16 + t - 64] = 1
            table[feature, MAIN + TAIL + position * 16 + 8 + t - 64] = 1
    return table


def dot(a, b, dims=(((1,), (0,)), ((), ()))):
    return lax.dot_general(a, b, dims, preferred_element_type=F32)


def iota(shape, dim):
    return lax.broadcasted_iota(jnp.int32, shape, dim)


def pick(source_row, n=256, m=256):
    return (source_row(iota((n, m), 0)) == iota((n, m), 1)).astype(F32).astype(BF)


def kernel(
    tok_hbm, mod_hbm, cot_hbm, wq_hbm, wo_hbm, table_hbm,
    out_hbm, outm_ref,
    raw, mod_ref, wq_ref, wo_ref,
    sa, ra, sb, rb, z, x80, x64, table, hid, hidp, gated, normed, inv, pr, acc, gp, gh_low, rr, rr2, sums, ms, mr,
    in_sem, out_sem, zh_s, zh_r, zl_s, zl_r, zc_s, zc_r, w_s, w_r, wc_s, wc_r,
    a_s, a_r, b_s, b_r, c_s, c_r, e_s, e_r, m_s, m_r,
):
    s, q = lax.axis_index("seq"), lax.axis_index("dp")
    y, x, zl = lax.rem(s, 4), lax.rem(s // 4, 4), s // 16
    zh, c = q // 2, lax.rem(q, 2)
    xy = x * 4 + y
    zfull = zh * 4 + zl

    def m4(v):
        return lax.rem(v + 8, 4)

    def dev(x_, y_, z_, c_):
        return ((lax.rem(z_, 4) * 4 + x_) * 4 + y_, (z_ // 4) * 2 + c_)

    def at_xy(k):
        return dev(m4(x + k // 4), m4(y + lax.rem(k, 4)), zfull, c)

    def at_zl(k):
        return dev(x, y, zh * 4 + m4(zl + k), c)

    def at_zh(k):
        return dev(x, y, m4(zh + k) * 4 + zl, c)

    def at_ring(k):
        return dev(x, y, lax.rem(zfull + k + 16, 16), c)

    other = dev(x, y, zfull, 1 - c)

    def copy(src, dst, ss, rs, to):
        return pltpu.make_async_remote_copy(
            src_ref=src, dst_ref=dst, send_sem=ss, recv_sem=rs, device_id=to, device_id_type=MESH
        )

    loads = [
        pltpu.make_async_copy(src, dst, in_sem.at[n])
        for n, (src, dst) in enumerate((
            (wq_hbm, wq_ref), (wo_hbm, wo_ref), (tok_hbm, raw.at[0]), (cot_hbm, raw.at[1]),
            (mod_hbm, mod_ref), (table_hbm, table),
        ))
    ]
    for load in loads:
        load.start()

    barrier = pltpu.get_barrier_semaphore()

    def greet(to):
        pl.semaphore_signal(barrier, inc=1, device_id=to, device_id_type=MESH)

    for k in (1, 2, 3):
        greet(at_zh(k))
        greet(at_zl(k))
    for k in (1, -1, 2, -2):
        greet(at_ring(k))
    greet(other)

    @pl.loop(1, 16)
    def _(k):
        greet(at_xy(k))

    loads[0].wait()
    loads[1].wait()
    wide = jnp.concatenate(
        [wq_ref[...].astype(F32), wo_ref[...].astype(F32), jnp.zeros((18, 64), F32)], axis=1
    )
    ends = [wide[16 + j:17 + j, 128 * m:128 * m + 128] for j in range(2) for m in range(5)]
    ends = jnp.concatenate(ends + [jnp.zeros((6, 128), F32)], axis=0)
    z[c, zl, zh] = jnp.concatenate([wide[:16], ends], axis=1).astype(BF)

    to_plane = pick(lambda o: ((o >> 3) & 1) * 128 + (o >> 4) * 8 + (o & 7))

    def first_order(n):
        loads[2 + n].wait()
        sa[n] = dot(to_plane, raw[n].reshape(256, D)).astype(BF).reshape(16, 16, D)

    first_order(0)
    pl.semaphore_wait(barrier, 26)

    def zh_copy(k):
        ref = z.at[c, zl, zh]
        return copy(ref, ref, zh_s.at[k], zh_r.at[k], at_zh(k))

    ring = (1, -1, 2)

    def zl_copy(n, group):
        ref = z.at[c, zl, group]
        return copy(ref, ref, zl_s.at[n, group], zl_r.at[n, group], at_ring(ring[n]))

    def zl_arrived(n, group):
        ref = z.at[c, m4(zl - ring[n]), group]
        copy(ref, ref, zl_s.at[n, group], zl_r.at[n, group], at_ring(ring[n])).wait_recv()

    def zc_copy(line, n):
        ref = z.at[c, line]
        return copy(ref, ref, zc_s.at[n], zc_r.at[n], other)

    for k in (2, 1, 3):
        zh_copy(k).start()
    for n in range(3):
        zl_copy(n, zh).start()

    def a_copy(n, k):
        return copy(sa.at[n, m4(x + k // 4) * 4 + m4(y + lax.rem(k, 4))], ra.at[n, xy],
                    a_s.at[n, k], a_r.at[n, k], at_xy(k))

    def a_send(n):
        @pl.loop(1, 16)
        def _(k):
            a_copy(n, k).start()

        ra[n, xy] = sa[n, xy]

    a_send(0)
    first_order(1)
    a_send(1)

    for k in (1, 3, 2):
        zh_copy(k).wait_recv()
        for n in range(3):
            zl_copy(n, m4(zh - k)).start()
    zc_copy(zl, 0).start()

    def b_copy(n, k):
        return copy(sb.at[n, m4(zl + k)], rb.at[n, zl], b_s.at[n, k], b_r.at[n, k], at_zl(k))

    to_line = pick(lambda o: ((o >> 2) & 15) * 16 + ((o >> 1) & 1) * 8 + (o >> 6) * 2 + (o & 1))

    def second_step(n):
        @pl.loop(1, 16)
        def _(k):
            a_copy(n, k).wait()

        sb[n] = dot(to_line, ra[n].reshape(256, D)).astype(BF).reshape(4, 64, D)
        for k in (2, 1, 3):
            b_copy(n, k).start()
        rb[n, zl] = sb[n, zl]

    for n in range(3):
        for k in range(4):
            zl_arrived(n, m4(zh - k))
        zc_copy(m4(zl - ring[n]), 1 + n).start()
    second_step(0)
    for n in range(4):
        ref = z.at[1 - c, m4(zl - (0, 1, -1, 2)[n])]
        copy(ref, ref, zc_s.at[n], zc_r.at[n], other).wait_recv()

    def block(d):
        parts = []
        for k in range(4):
            stored = z[d % 2, k, d // 2].astype(F32)
            parts.append(stored[:, :640])
            for j in range(2):
                parts.append(jnp.concatenate(
                    [stored[5 * j + m:5 * j + m + 1, 640:768] for m in range(5)], axis=1
                ))
        return jnp.concatenate(parts, axis=0)

    blocks = [block(d) for d in range(8)]
    full = jnp.concatenate([b[:, :432] for b in blocks] + [b[:, 432:576] for b in blocks], axis=1)
    quarters = [full[:, k * D:(k + 1) * D] for k in range(4)]
    x80[0, xy, 0:64, :] = quarters[0][:64].astype(BF)
    x80[0, xy, 64:80, :] = jnp.concatenate([quarters[0][64:], quarters[1][64:]], axis=0).astype(BF)
    x64[0, xy] = quarters[1][:64].astype(BF)
    x80[1, xy, 0:64, :] = quarters[3][:64].astype(BF)
    x80[1, xy, 64:80, :] = jnp.concatenate([quarters[2][64:], quarters[3][64:]], axis=0).astype(BF)
    x64[1, xy] = quarters[2][:64].astype(BF)

    stores = (x80, x64)
    first_axis = (((1 - c), c), (c, (1 - c)))

    def shifted(st, i, j):
        fx, fy = first_axis[st]
        return m4(x + i * fx + j * fy), m4(y + i * fy + j * fx)

    def position(st, i, j):
        px, py = shifted(st, i, j)
        return px * 4 + py

    sent = []

    def w_send(st, i, j, to_i, to_j):
        ref = stores[st].at[c, position(st, i, j)]
        px, py = shifted(st, to_i, to_j)
        index = ((i - to_i) % 4) * 4 + (j - to_j) % 4
        cp = copy(ref, ref, w_s.at[st, index], w_r.at[st, index], dev(px, py, zfull, c))
        cp.start()
        sent.append(cp)

    def w_arrived(st, i, j):
        ref = stores[st].at[c, position(st, i, j)]
        index = i * 4 + j
        copy(ref, ref, w_s.at[st, index], w_r.at[st, index], other).wait_recv()
        cp = copy(ref, ref, wc_s.at[st, index], wc_r.at[st, index], other)
        cp.start()
        sent.append(cp)

    def w_both_ways(st, i):
        w_send(st, i, 0, 0, 1)
        w_send(st, i, 0, 0, -1)

    def w_sides(st, i):
        w_arrived(st, i, 3)
        if i in (0, 2):
            w_send(st, i, 3, 0, 1)
        w_arrived(st, i, 1)
        if i in (1, 3):
            w_send(st, i, 1, 0, -1)

    for st in range(2):
        for i in (1, -1, 2):
            w_send(st, 0, 0, i, 0)
        w_both_ways(st, 0)

    second_step(1)
    for i in (1, 3):
        for st in range(2):
            w_arrived(st, i, 0)
            w_both_ways(st, i)
    for st in range(2):
        w_sides(st, 0)
    for st in range(2):
        w_arrived(st, 2, 0)
        w_both_ways(st, 2)

    for n in (0, 1):
        for k in (1, 2, 3):
            b_copy(n, k).wait()
    loads[4].wait()
    loads[5].wait()

    def clip_of(rows_shape):
        return ((iota(rows_shape, 0) >> 1) & 1) == 1

    def norm_rows(i):
        rows = pl.ds(pl.multiple_of(i * 32, 32), 32)
        tile = rb.at[0, i // 2][pl.ds(pl.multiple_of(lax.rem(i, 2) * 32, 32), 32), :].astype(F32)
        cot = rb.at[1, i // 2][pl.ds(pl.multiple_of(lax.rem(i, 2) * 32, 32), 32), :].astype(F32)
        mean = jnp.sum(tile, axis=1, keepdims=True) * (1.0 / D)
        centred = tile - mean
        inv_std = lax.rsqrt(jnp.sum(centred * centred, axis=1, keepdims=True) * (1.0 / D) + EPS)
        nrm = centred * inv_std
        normed[rows, :] = nrm
        inv[rows, :] = jnp.broadcast_to(inv_std, (32, 128))
        second = clip_of((32, D))
        shift = jnp.where(second, mod_ref[0, 1:2, :], mod_ref[0, 0:1, :])
        scale = jnp.where(second, mod_ref[1, 1:2, :], mod_ref[1, 0:1, :])
        gate = jnp.where(second, mod_ref[2, 1:2, :], mod_ref[2, 0:1, :])
        hid[rows, :] = (nrm * (1.0 + scale) + shift).astype(BF)
        gated[rows, :] = (cot * gate).astype(BF)

    pl.loop(0, 8)(norm_rows)
    hidp[...] = dot(hid[...], table[...]).astype(BF)

    for i in (1, 3, 2):
        for st in range(2):
            w_sides(st, i)
    for i in range(4):
        for st in range(2):
            w_arrived(st, i, 2)
    for k in range(1, 16):
        for st in range(2):
            ref = stores[st].at[1 - c, position(1 - st, k // 4, k % 4)]
            copy(ref, ref, wc_s.at[st, k], wc_r.at[st, k], other).wait_recv()
    for cp in sent:
        cp.wait_send()
    for k in (1, 2, 3):
        zh_copy(k).wait_send()
    for n in range(3):
        for k in range(4):
            zl_copy(n, m4(zh - k)).wait_send()
    for n in range(4):
        zc_copy(m4(zl - (0, 1, -1, 2)[n]), n).wait_send()

    def main_rows(ref, core, cols=slice(None)):
        return ref[core, :, 0:64, cols].reshape(MAIN, -1)

    def tail_rows(core, cols=slice(None)):
        return x80[core, :, 64:80, cols].reshape(TAIL, -1)

    first, second_half = pl.ds(MAIN, TAIL), pl.ds(MAIN + TAIL, TAIL)

    def project(i):
        cols = pl.ds(pl.multiple_of(i * 384, 128), 384)
        main = hidp[:, 0:MAIN]
        pr[0, :, cols] = (dot(main, main_rows(x80, 0, cols)) + dot(hidp[:, first], tail_rows(0, cols))).astype(BF)
        pr[1, :, cols] = (dot(main, main_rows(x64, 0, cols)) + dot(hidp[:, second_half], tail_rows(0, cols))).astype(BF)
        pr[2, :, cols] = (dot(main, main_rows(x64, 1, cols)) + dot(hidp[:, first], tail_rows(1, cols))).astype(BF)

    pl.loop(0, 3)(project)
    ga = dot(gated[...], main_rows(x80, 1), RHS_T).astype(BF)
    ga_tail = dot(gated[...], tail_rows(1), RHS_T).astype(BF)
    pr[3] = (dot(ga, table[:, 0:MAIN], RHS_T) + dot(ga_tail, table[:, second_half], RHS_T)).astype(BF)

    acc[...] = jnp.zeros_like(acc)
    score_scale = 1.0 / math.sqrt(HD)
    same = (iota((256, 256), 0) & 3) == (iota((256, 256), 1) & 3)

    def head(i):
        first = jnp.minimum((i * HD) // 128, 7)
        cols = pl.ds(pl.multiple_of(first * 128, 128), 256)
        lane = iota((256, 256), 1) - (i * HD - first * 128)
        inside = (lane >= 0) & (lane < HD)
        zero = jnp.zeros((256, 256), BF)
        query = jnp.where(inside, pr[0, :, cols], zero)
        keys = jnp.where(inside, pr[1, :, cols], zero)
        values = pr[2, :, cols]
        grad = jnp.where(inside, pr[3, :, cols], zero)
        scores = dot(keys, query, RHS_T) * score_scale
        e = jnp.exp(jnp.where(same, scores, -jnp.inf))
        probs = e * (1.0 / jnp.sum(e, axis=0, keepdims=True))
        grad_probs = dot(values, grad, RHS_T)
        inner = jnp.sum(probs * grad_probs, axis=0, keepdims=True)
        grad_scores = (probs * (grad_probs - inner) * score_scale).astype(BF)
        acc[0, :, cols] += dot(grad_scores, keys, LHS_T)
        acc[1, :, cols] += dot(grad_scores, query)
        acc[2, :, cols] += dot(probs.astype(BF), grad)

    pl.loop(0, H)(head)
    for k in range(3):
        gp[k] = acc[k].astype(BF)

    gq, gk, gv = gp[0], gp[1], gp[2]
    back_main = (
        dot(gq, main_rows(x80, 0), RHS_T) + dot(gk, main_rows(x64, 0), RHS_T) + dot(gv, main_rows(x64, 1), RHS_T)
    )
    back_first = dot(gq, tail_rows(0), RHS_T) + dot(gv, tail_rows(1), RHS_T)
    back_second = dot(gk, tail_rows(0), RHS_T)
    for part, lanes in ((back_main, pl.ds(0, MAIN)), (back_first, first), (back_second, second_half)):
        top = part.astype(BF)
        hidp[:, lanes] = top
        gh_low[:, lanes] = (part - top.astype(F32)).astype(BF)
    acc[2] = dot(hidp[...], table[...], RHS_T) + dot(gh_low[...], table[...], RHS_T)

    sums[...] = jnp.zeros_like(sums)

    def norm_back(i):
        rows = pl.ds(pl.multiple_of(i * 32, 32), 32)
        inside = pl.ds(pl.multiple_of(lax.rem(i, 2) * 32, 32), 32)
        gh = acc[2, rows, :]
        nrm = normed[rows, :]
        second = clip_of((32, D))
        zero = jnp.zeros_like(gh)
        cross = gh * nrm
        sums[0:1, :] += jnp.sum(jnp.where(second, zero, gh), axis=0, keepdims=True)
        sums[1:2, :] += jnp.sum(jnp.where(second, zero, cross), axis=0, keepdims=True)
        sums[2:3, :] += jnp.sum(jnp.where(second, gh, zero), axis=0, keepdims=True)
        sums[3:4, :] += jnp.sum(jnp.where(second, cross, zero), axis=0, keepdims=True)
        gn = gh * (1.0 + jnp.where(second, mod_ref[1, 1:2, :], mod_ref[1, 0:1, :]))
        mean_grad = jnp.sum(gn, axis=1, keepdims=True) * (1.0 / D)
        mean_cross = jnp.sum(gn * nrm, axis=1, keepdims=True) * (1.0 / D)
        cot = rb.at[1, i // 2][inside, :].astype(F32)
        gt = cot + inv[rows, 0:1] * (gn - mean_grad - nrm * mean_cross)
        rr.at[0, i // 2][inside, :] = gt.astype(BF)

    pl.loop(0, 8)(norm_back)

    ms[0, 0:4, :] = sums[0:4, 0:640]
    ms[0, 4:8, 0:512] = sums[0:4, 640:1152]
    ms[0, 4:8, 512:640] = jnp.zeros((4, 128), F32)
    places = (zl, x, y)

    def m_copy(step, k):
        to = (at_zl(k), dev(m4(x + k), y, zfull, c), dev(x, m4(y + k), zfull, c))[step]
        return copy(ms.at[step], mr.at[step, places[step]], m_s.at[step, k], m_r.at[step, k], to)

    def m_start(step):
        for k in (1, 2, 3):
            m_copy(step, k).start()
        mr[step, places[step]] = ms[step]

    def m_sum(step):
        for k in (1, 2, 3):
            m_copy(step, k).wait()
        return ((mr[step, 0] + mr[step, 1]) + mr[step, 2]) + mr[step, 3]

    m_start(0)
    pieces = (pl.ds(0, 640), pl.ds(640, 512))

    def back_copy(n, k):
        return copy(rr.at[0, m4(zl + k), :, pieces[n]], rr.at[1, zl, :, pieces[n]], c_s.at[n, k], c_r.at[n, k], at_zl(k))

    for n in range(2):
        for k in (2, 1, 3):
            back_copy(n, k).start()
    rr[1, zl] = rr[0, zl]
    ms[1] = m_sum(0)
    m_start(1)

    from_line = pick(lambda o: ((o >> 1) & 3) * 64 + (o >> 4) * 4 + ((o >> 3) & 1) * 2 + (o & 1))

    def e_copy(n, k):
        return copy(rr2.at[0, m4(x + k // 4) * 4 + m4(y + lax.rem(k, 4)), :, pieces[n]],
                    rr2.at[1, xy, :, pieces[n]], e_s.at[n, k], e_r.at[n, k], at_xy(k))

    for n in range(2):
        for k in (1, 2, 3):
            back_copy(n, k).wait()
        lanes = pieces[n]
        rr2[0, :, :, lanes] = dot(from_line, rr[1, :, :, lanes].reshape(256, -1)).astype(BF).reshape(16, 16, -1)

        @pl.loop(1, 16)
        def _(k, n=n):
            e_copy(n, k).start()

        if n == 0:
            ms[2] = m_sum(1)
            m_start(2)

    rr2[1, xy] = rr2[0, xy]
    outm_ref[...] = m_sum(2)
    for n in range(2):
        @pl.loop(1, 16)
        def _(k, n=n):
            e_copy(n, k).wait()

    store = pltpu.make_async_copy(rr2.at[1], out_hbm, out_sem)
    store.start()
    store.wait()


def local(tokens, modulation, cotangent, qkv_weight, out_weight):
    table = jnp.asarray(place_table(), BF)
    hbm = pl.BlockSpec(memory_space=pl.ANY)
    dma = pltpu.SemaphoreType.DMA
    vmem = pltpu.VMEM
    rows, sums = pl.pallas_call(
        kernel,
        out_shape=(
            jax.ShapeDtypeStruct((16, 16, D), BF),
            jax.ShapeDtypeStruct((8, 640), F32),
        ),
        in_specs=[hbm] * 6,
        out_specs=(hbm, pl.BlockSpec(memory_space=pltpu.VMEM)),
        scratch_shapes=[
            vmem((2, 2, 128, D), BF),
            vmem((3, 2, D), F32),
            vmem((18, 432), BF),
            vmem((18, 144), BF),
            vmem((2, 16, 16, D), BF),
            vmem((2, 16, 16, D), BF),
            vmem((2, 4, 64, D), BF),
            vmem((2, 4, 64, D), BF),
            vmem((2, 4, 4, 16, 768), BF),
            vmem((2, 16, 80, D), BF),
            vmem((2, 16, 64, D), BF),
            vmem((D, MAIN + 2 * TAIL), BF),
            vmem((256, D), BF),
            vmem((256, MAIN + 2 * TAIL), BF),
            vmem((256, D), BF),
            vmem((256, D), F32),
            vmem((256, 128), F32),
            vmem((4, 256, D), BF),
            vmem((3, 256, D), F32),
            vmem((3, 256, D), BF),
            vmem((256, MAIN + 2 * TAIL), BF),
            vmem((2, 4, 64, D), BF),
            vmem((2, 16, 16, D), BF),
            vmem((8, D), F32),
            vmem((3, 8, 640), F32),
            vmem((3, 4, 8, 640), F32),
            dma((6,)), dma,
            dma((4,)), dma((4,)), dma((3, 4)), dma((3, 4)), dma((4,)), dma((4,)),
            dma((2, 16)), dma((2, 16)), dma((2, 16)), dma((2, 16)),
            dma((2, 16)), dma((2, 16)), dma((2, 4)), dma((2, 4)),
            dma((2, 4)), dma((2, 4)), dma((2, 16)), dma((2, 16)),
            dma((3, 4)), dma((3, 4)),
        ],
        compiler_params=pltpu.CompilerParams(
            collective_id=0, has_side_effects=True, vmem_limit_bytes=60 * 1024 * 1024
        ),
        name="sublayer_backward",
    )(
        tokens.reshape(2, 128, D), modulation.transpose(1, 0, 2), cotangent.reshape(2, 128, D),
        qkv_weight, out_weight, table,
    )
    grad_tokens = rows.reshape(16, 2, 8, D).transpose(1, 0, 2, 3).reshape(2, 1, 128, D)
    grad_modulation = jnp.concatenate([sums[0:4, :], sums[4:8, :512]], axis=1).reshape(2, 2, D)
    return grad_tokens, grad_modulation


def solution(mesh):
    in_specs = (
        P("dp", "seq", None, None),
        P("dp", None, None),
        P("dp", "seq", None, None),
        P("seq", "dp"),
        P("seq", "dp"),
    )
    out_specs = (P("dp", "seq", None, None), P("dp", None, None))
    return jax.shard_map(local, mesh=mesh, in_specs=in_specs, out_specs=out_specs, check_vma=False)
```

time: 148 us -> 124 us (0.84)
  Pallas kernels: 142 us -> 118 us
    pallas_call x1, Pallas kernels: 142 us -> 118 us  [local(): pl.pallas_call(kernel, out_shape=(jax.ShapeDtypeStruct((16, 16, D), BF),...]
    unnamed x3 -> x0, local copies, waits for them, and re-layouts: 4.62 us -> none
    reshape x0 -> x2, local copies, waits for them, and re-layouts: none -> 2.55 us  [the longest x1 1.92 us: local(): rows.reshape(16, 2, 8, D).transpose(1, 0, 2, 3).reshape(2, 1, 128, D)]
where the time goes in v2:
time: 124 us; the launch traced here: 123 us
  Pallas kernels  118 us (95%)
  local copies, waits for them, and re-layouts  4 us (3%)
    pallas_call x1, Pallas kernels, local(): pl.pallas_call(kernel, out_shape=(jax.ShapeDtypeStruct((16, 16, D), BF),...  118 us

profile of v2, /device:TPU:1, one launch (start us, length us, event | category | flops | bytes accessed | tf_op | source)
XLA Modules:
  0.0 123.1 jit_solution(11668722939763622852)
XLA Ops:
  0.6 118.4 %sublayer_backward.1 = (bf16[16,16,1152]{2,1,0:T(8,128)(2,1)}, f32[8,640]{1,0:T(8,128)}) custom-call(bf16[2,128,1152]{2,1,0:T(8,128)(2,1)} %bitcast.10, f32[3,2,1152]{2,1,0:T(2,128)} %bitcast.12, bf16[2,128,1152]{2,1,0:T(8,128)(2,1)} %bitcast.11, bf16[18,432]{1,0:T(8,128)(2,1)} %wq_hbm.1, bf16[18,144]{1,0:T(8,128)(2,1)} %wo_hbm.1, ...), custom_call_target="tpu_custom_call" | custom-call | tf_op jit(solution)/shard_map/sublayer_backward/pallas_call | solution.py:482
  119.1 0.7 slice.6
  119.8 0.7 slice.7
  120.5 0.6 reshape.23
  121.1 1.9 %copy_bitcast_fusion = bf16[2,1,128,1152]{3,2,1,0:T(8,128)(2,1)} fusion(bf16[16,16,1152]{2,1,0:T(8,128)(2,1)} %get-tuple-element.4), kind=kLoop, calls=%fused_computation | loop fusion | bytes 1179648 | tf_op jit(solution)/shard_map/reshape | solution.py:532
  (1 shorter events, 0.0 us)

commit v3 on v2

v3 whole, which is shorter than its diff:
```python
import functools
import math

import jax
import jax.numpy as jnp
import numpy as np
from jax import lax
from jax.experimental import pallas as pl
from jax.experimental.pallas import tpu as pltpu
from jax.sharding import PartitionSpec as P

D = 1152
H = 16
PAIRS_AT_ONCE = 8
HD = 72
EPS = 1e-06
MESH = pl.DeviceIdType.MESH
BF = jnp.bfloat16
F32 = jnp.float32
RHS_T = (((1,), (1,)), ((), ()))
LHS_T = (((0,), (0,)), ((), ()))


MAIN, TAIL = 1024, 256


def place_table():
    table = np.zeros((MAIN + 2 * TAIL, D), np.float32)
    for feature in range(D):
        zl, rest = divmod(feature, 288)
        position, i = divmod(rest, 18)
        t = zl * 18 + i
        if t < 64:
            table[position * 64 + t, feature] = 1
        else:
            table[MAIN + position * 16 + t - 64, feature] = 1
            table[MAIN + TAIL + position * 16 + 8 + t - 64, feature] = 1
    return table


def dot(a, b, dims=(((1,), (0,)), ((), ()))):
    return lax.dot_general(a, b, dims, preferred_element_type=F32)


def iota(shape, dim):
    return lax.broadcasted_iota(jnp.int32, shape, dim)


def pick(source_row, n=256, m=256):
    return (source_row(iota((n, m), 0)) == iota((n, m), 1)).astype(F32).astype(BF)


def kernel(
    tok_hbm, mod_hbm, cot_hbm, wq_hbm, wo_hbm, table_hbm,
    out_hbm, outm_ref,
    raw, mod_ref, wq_ref, wo_ref,
    sa, ra, sb, rb, z, x80, x64, table, hid, hidg, hidt, gated, normed, inv, acc, pr, heads_acc, gp, gh_rows, gh, rr, rr2, out, ms, mr,
    in_sem, out_sem, zh_s, zh_r, zl_s, zl_r, zc_s, zc_r, w_s, w_r, wc_s, wc_r,
    a_s, a_r, b_s, b_r, c_s, c_r, e_s, e_r, m_s, m_r,
):
    s, q = lax.axis_index("seq"), lax.axis_index("dp")
    y, x, zl = lax.rem(s, 4), lax.rem(s // 4, 4), s // 16
    zh, c = q // 2, lax.rem(q, 2)
    xy = x * 4 + y
    zfull = zh * 4 + zl

    def m4(v):
        return lax.rem(v + 8, 4)

    def dev(x_, y_, z_, c_):
        return ((lax.rem(z_, 4) * 4 + x_) * 4 + y_, (z_ // 4) * 2 + c_)

    def at_xy(k):
        return dev(m4(x + k // 4), m4(y + lax.rem(k, 4)), zfull, c)

    def at_zl(k):
        return dev(x, y, zh * 4 + m4(zl + k), c)

    def at_zh(k):
        return dev(x, y, m4(zh + k) * 4 + zl, c)

    def at_ring(k):
        return dev(x, y, lax.rem(zfull + k + 16, 16), c)

    other = dev(x, y, zfull, 1 - c)

    def copy(src, dst, ss, rs, to):
        return pltpu.make_async_remote_copy(
            src_ref=src, dst_ref=dst, send_sem=ss, recv_sem=rs, device_id=to, device_id_type=MESH
        )

    loads = [
        pltpu.make_async_copy(src, dst, in_sem.at[n])
        for n, (src, dst) in enumerate((
            (wq_hbm, wq_ref), (wo_hbm, wo_ref), (tok_hbm, raw.at[0]), (cot_hbm, raw.at[1]),
            (mod_hbm, mod_ref), (table_hbm, table),
        ))
    ]
    for load in loads:
        load.start()

    barrier = pltpu.get_barrier_semaphore()

    def greet(to):
        pl.semaphore_signal(barrier, inc=1, device_id=to, device_id_type=MESH)

    for k in (1, 2, 3):
        greet(at_zh(k))
        greet(at_zl(k))
    for k in (1, -1, 2, -2):
        greet(at_ring(k))
    greet(other)

    @pl.loop(1, 16)
    def _(k):
        greet(at_xy(k))

    loads[0].wait()
    loads[1].wait()
    wide = jnp.concatenate(
        [wq_ref[...].astype(F32), wo_ref[...].astype(F32), jnp.zeros((18, 64), F32)], axis=1
    )
    ends = [wide[16 + j:17 + j, 128 * m:128 * m + 128] for j in range(2) for m in range(5)]
    ends = jnp.concatenate(ends + [jnp.zeros((6, 128), F32)], axis=0)
    z[c, zl, zh] = jnp.concatenate([wide[:16], ends], axis=1).astype(BF)

    to_plane = pick(lambda o: ((o >> 3) & 1) * 128 + (o >> 4) * 8 + (o & 7))

    def first_order(n):
        loads[2 + n].wait()
        sa[n] = dot(to_plane, raw[n].reshape(256, D)).astype(BF).reshape(16, 16, D)

    first_order(0)
    pl.semaphore_wait(barrier, 26)

    def zh_copy(k):
        ref = z.at[c, zl, zh]
        return copy(ref, ref, zh_s.at[k], zh_r.at[k], at_zh(k))

    ring = (1, -1, 2)

    def zl_copy(n, group):
        ref = z.at[c, zl, group]
        return copy(ref, ref, zl_s.at[n, group], zl_r.at[n, group], at_ring(ring[n]))

    def zl_arrived(n, group):
        ref = z.at[c, m4(zl - ring[n]), group]
        copy(ref, ref, zl_s.at[n, group], zl_r.at[n, group], at_ring(ring[n])).wait_recv()

    def zc_copy(line, n):
        ref = z.at[c, line]
        return copy(ref, ref, zc_s.at[n], zc_r.at[n], other)

    for k in (2, 1, 3):
        zh_copy(k).start()
    for n in range(3):
        zl_copy(n, zh).start()

    def a_copy(n, k):
        return copy(sa.at[n, m4(x + k // 4) * 4 + m4(y + lax.rem(k, 4))], ra.at[n, xy],
                    a_s.at[n, k], a_r.at[n, k], at_xy(k))

    def a_send(n):
        @pl.loop(1, 16)
        def _(k):
            a_copy(n, k).start()

        ra[n, xy] = sa[n, xy]

    a_send(0)
    first_order(1)
    a_send(1)

    for k in (1, 3, 2):
        zh_copy(k).wait_recv()
        for n in range(3):
            zl_copy(n, m4(zh - k)).start()
    zc_copy(zl, 0).start()

    def b_copy(n, k):
        return copy(sb.at[n, m4(zl + k)], rb.at[n, zl], b_s.at[n, k], b_r.at[n, k], at_zl(k))

    to_line = pick(lambda o: ((o >> 1) & 15) * 16 + ((o >> 5) & 1) * 8 + (o >> 6) * 2 + (o & 1))

    def second_step(n):
        @pl.loop(1, 16)
        def _(k):
            a_copy(n, k).wait()

        sb[n] = dot(to_line, ra[n].reshape(256, D)).astype(BF).reshape(4, 64, D)
        for k in (2, 1, 3):
            b_copy(n, k).start()
        rb[n, zl] = sb[n, zl]

    second_step(0)
    for n in range(3):
        for k in range(4):
            zl_arrived(n, m4(zh - k))
        zc_copy(m4(zl - ring[n]), 1 + n).start()
    for n in range(4):
        ref = z.at[1 - c, m4(zl - (0, 1, -1, 2)[n])]
        copy(ref, ref, zc_s.at[n], zc_r.at[n], other).wait_recv()

    def block(d):
        parts = []
        for k in range(4):
            stored = z[d % 2, k, d // 2].astype(F32)
            parts.append(stored[:, :640])
            for j in range(2):
                parts.append(jnp.concatenate(
                    [stored[5 * j + m:5 * j + m + 1, 640:768] for m in range(5)], axis=1
                ))
        return jnp.concatenate(parts, axis=0)

    blocks = [block(d) for d in range(8)]
    full = jnp.concatenate([b[:, :432] for b in blocks] + [b[:, 432:576] for b in blocks], axis=1)
    quarters = [full[:, k * D:(k + 1) * D] for k in range(4)]
    x80[0, x, y, 0:64, :] = quarters[0][:64].astype(BF)
    x80[0, x, y, 64:80, :] = jnp.concatenate([quarters[0][64:], quarters[1][64:]], axis=0).astype(BF)
    x64[0, x, y] = quarters[1][:64].astype(BF)
    x80[1, x, y, 0:64, :] = quarters[3][:64].astype(BF)
    x80[1, x, y, 64:80, :] = jnp.concatenate([quarters[2][64:], quarters[3][64:]], axis=0).astype(BF)
    x64[1, x, y] = quarters[2][:64].astype(BF)

    stores = (x80, x64)
    first_axis = (((1 - c), c), (c, (1 - c)))

    def shifted(st, i, j):
        fx, fy = first_axis[st]
        return m4(x + i * fx + j * fy), m4(y + i * fy + j * fx)

    def held(st, i, j):
        px, py = shifted(st, i, j)
        return stores[st].at[c, px, py]

    sent = []

    def w_send(st, i, j, to_i, to_j):
        ref = held(st, i, j)
        px, py = shifted(st, to_i, to_j)
        index = ((i - to_i) % 4) * 4 + (j - to_j) % 4
        cp = copy(ref, ref, w_s.at[st, index], w_r.at[st, index], dev(px, py, zfull, c))
        cp.start()
        sent.append(cp)

    def w_arrived(st, i, j):
        ref = held(st, i, j)
        index = i * 4 + j
        copy(ref, ref, w_s.at[st, index], w_r.at[st, index], other).wait_recv()
        cp = copy(ref, ref, wc_s.at[st, index], wc_r.at[st, index], other)
        cp.start()
        sent.append(cp)

    def w_both_ways(st, i):
        w_send(st, i, 0, 0, 1)
        w_send(st, i, 0, 0, -1)

    def w_sides(st, i):
        w_arrived(st, i, 3)
        if i in (0, 2):
            w_send(st, i, 3, 0, 1)
        w_arrived(st, i, 1)
        if i in (1, 3):
            w_send(st, i, 1, 0, -1)

    for st in range(2):
        for i in (1, -1, 2):
            w_send(st, 0, 0, i, 0)
        w_both_ways(st, 0)

    second_step(1)
    for i in (1, 3):
        for st in range(2):
            w_arrived(st, i, 0)
            w_both_ways(st, i)
    for st in range(2):
        w_sides(st, 0)
    for st in range(2):
        w_arrived(st, 2, 0)
        w_both_ways(st, 2)

    def places_of(i):
        clip, line = lax.rem(i, 2), i // 2
        rows = pl.ds(pl.multiple_of(clip * 128 + line * 32, 32), 32)
        return clip, line, rows, pl.ds(pl.multiple_of(clip * 32, 32), 32)

    def norm_rows(i):
        clip, line, rows, source = places_of(i)
        tile = rb.at[0, line][source, :].astype(F32)
        mean = jnp.sum(tile, axis=1, keepdims=True) * (1.0 / D)
        centred = tile - mean
        inv_std = lax.rsqrt(jnp.sum(centred * centred, axis=1, keepdims=True) * (1.0 / D) + EPS)
        nrm = centred * inv_std
        normed[rows, :] = nrm
        inv[rows, :] = jnp.broadcast_to(inv_std, (32, 128))
        hid[rows, :] = (nrm * (1.0 + mod_ref[1, pl.ds(clip, 1), :]) + mod_ref[0, pl.ds(clip, 1), :]).astype(BF)

    def gate_rows(i):
        clip, line, rows, source = places_of(i)
        cot = rb.at[1, line][source, :].astype(F32)
        gated[rows, :] = (cot * mod_ref[2, pl.ds(clip, 1), :]).astype(BF)

    def hidden_in(places):
        return dot(hid[...], places, RHS_T).astype(BF)

    def table_column(yj):
        return jnp.concatenate(
            [table[pl.ds(pl.multiple_of((k * 4 + yj) * 64, 64), 64), :] for k in range(4)], axis=0
        )

    def table_row(xj):
        return table[pl.ds(pl.multiple_of(xj * 256, 256), 256), :]

    def project(j, last=False):
        xj, yj = m4(x + j), m4(y + j)

        def columns(i):
            cols = pl.ds(pl.multiple_of(i * 384, 128), 384)
            sums_now = [
                dot(hidg[j, 0], x80[0, :, yj, 0:64, cols].reshape(256, 384)),
                dot(hidg[j, 1], x64[0, xj, :, :, cols].reshape(256, 384)),
                dot(hidg[j, 0], x64[1, :, yj, :, cols].reshape(256, 384)),
            ]
            for k in range(3):
                if j == 0:
                    acc[k, :, cols] = sums_now[k]
                elif not last:
                    acc[k, :, cols] += sums_now[k]
                else:
                    tail = x80[k // 2, :, :, 64:80, cols].reshape(TAIL, 384)
                    pr[k, :, cols] = (acc[k, :, cols] + sums_now[k] + dot(hidt[k % 2], tail)).astype(BF)

        pl.loop(0, 3)(columns)

    def project_grad(j, last=False):
        xj = m4(x + j)
        ga = dot(gated[...], x80[1, xj, :, 0:64, :].reshape(256, D), RHS_T).astype(BF)
        now = dot(ga, table_row(xj))
        if j == 0:
            acc[3] = now
        elif not last:
            acc[3] += now
        else:
            ga = dot(gated[...], x80[1, :, :, 64:80, :].reshape(TAIL, D), RHS_T).astype(BF)
            pr[3] = (acc[3] + now + dot(ga, table[MAIN + TAIL:MAIN + 2 * TAIL, :])).astype(BF)

    def w_across(i, j):
        for st in range(2):
            px, py = shifted(1 - st, i, j)
            ref = stores[st].at[1 - c, px, py]
            index = i * 4 + j
            copy(ref, ref, wc_s.at[st, index], wc_r.at[st, index], other).wait_recv()

    for k in (1, 2, 3):
        b_copy(0, k).wait()
    for load in loads[4:]:
        load.wait()
    pl.loop(0, 8)(norm_rows)
    for k in range(2):
        hidt[k] = hidden_in(table[MAIN + k * TAIL:MAIN + (k + 1) * TAIL, :])
    for j in range(4):
        hidg[j, 0] = hidden_in(table_column(m4(y + j)))
        hidg[j, 1] = hidden_in(table_row(m4(x + j)))
    for st in range(2):
        w_sides(st, 1)
    for i in (1, 2, 3):
        w_across(i, 0)
    project(0)
    for i in (3, 2):
        for st in range(2):
            w_sides(st, i)
    for j in (3, 1):
        for i in range(4):
            w_across(i, j)
        project(j)
    for k in (1, 2, 3):
        b_copy(1, k).wait()
    pl.loop(0, 8)(gate_rows)
    for j in (0, 3, 1):
        project_grad(j)
    for i in range(4):
        for st in range(2):
            w_arrived(st, i, 2)
    for i in range(4):
        w_across(i, 2)
    project(2, last=True)
    project_grad(2, last=True)
    for cp in sent:
        cp.wait_send()
    for k in (1, 2, 3):
        zh_copy(k).wait_send()
    for n in range(3):
        for k in range(4):
            zl_copy(n, m4(zh - k)).wait_send()
    for n in range(4):
        zc_copy(m4(zl - (0, 1, -1, 2)[n]), n).wait_send()

    def main_rows(ref, core):
        return ref[core, :, :, 0:64, :].reshape(MAIN, D)

    def tail_rows(core):
        return x80[core, :, :, 64:80, :].reshape(TAIL, D)

    score_scale = 1.0 / math.sqrt(HD)
    same = (iota((128, 256), 0) & 1) == (iota((128, 256), 1) & 1)

    def attend(clip):
        rows = pl.ds(clip * 128, 128)
        heads_acc[...] = jnp.zeros_like(heads_acc)

        def head_pair(i):
            first = (i * 2 * HD) // 128
            cols = pl.ds(pl.multiple_of(first * 128, 128), 256)
            lane = iota((128, 256), 1) - (i * 2 * HD - first * 128)
            zero = jnp.zeros((128, 256), BF)

            def by_head(window):
                return jnp.concatenate([
                    jnp.where((lane >= 0) & (lane < HD), window, zero),
                    jnp.where((lane >= HD) & (lane < 2 * HD), window, zero),
                ], axis=0)

            keys, values = pr[1, rows, cols], pr[2, rows, cols]
            queries, grads = by_head(pr[0, rows, cols]), by_head(pr[3, rows, cols])
            scores = dot(keys, queries, RHS_T) * score_scale
            e = jnp.exp(jnp.where(same, scores, -jnp.inf))
            probs = e * (1.0 / jnp.sum(e, axis=0, keepdims=True))
            grad_probs = dot(values, grads, RHS_T)
            inner = jnp.sum(probs * grad_probs, axis=0, keepdims=True)
            grad_scores = (probs * (grad_probs - inner) * score_scale).astype(BF)
            upright = jnp.concatenate([grad_scores[:, 0:128], grad_scores[:, 128:256]], axis=0)
            heads_acc[0, :, cols] += dot(upright, by_head(keys), LHS_T)
            heads_acc[1, :, cols] += dot(grad_scores, queries)
            heads_acc[2, :, cols] += dot(probs.astype(BF), grads)

        pl.loop(0, H // 2, unroll=PAIRS_AT_ONCE)(head_pair)
        for k in range(3):
            gp[k] = heads_acc[k].astype(BF)

    def back_rows(clip):
        gq, gk, gv = gp[0], gp[1], gp[2]
        gh_rows[:, 0:MAIN] = (
            dot(gq, main_rows(x80, 0), RHS_T) + dot(gk, main_rows(x64, 0), RHS_T) + dot(gv, main_rows(x64, 1), RHS_T)
        ).astype(BF)
        tails = dot(gp[0:2].reshape(256, D), tail_rows(0), RHS_T)
        gh_rows[:, MAIN:MAIN + TAIL] = (tails[0:128] + dot(gv, tail_rows(1), RHS_T)).astype(BF)
        gh_rows[:, MAIN + TAIL:MAIN + 2 * TAIL] = tails[128:256].astype(BF)
        gh[...] = dot(gh_rows[...], table[...])

        shift_sum = jnp.sum(gh[...], axis=0, keepdims=True)
        scale_sum = jnp.sum(gh[...] * normed[clip * 128:clip * 128 + 128, :], axis=0, keepdims=True)
        for n, row in enumerate((shift_sum, scale_sum)):
            n += 2 * clip
            ms[0, n:n + 1, :] = row[:, 0:640]
            ms[0, n + 4:n + 5, 0:512] = row[:, 640:1152]
            ms[0, n + 4:n + 5, 512:640] = jnp.zeros((1, 128), F32)
        if clip == 1:
            m_start(0)

        def norm_back(line):
            rows = pl.ds(pl.multiple_of(clip * 128 + line * 32, 32), 32)
            grad_hidden = gh[pl.ds(pl.multiple_of(line * 32, 32), 32), :]
            nrm = normed[rows, :]
            gn = grad_hidden * (1.0 + mod_ref[1, clip:clip + 1, :])
            mean_grad = jnp.sum(gn, axis=1, keepdims=True) * (1.0 / D)
            mean_cross = jnp.sum(gn * nrm, axis=1, keepdims=True) * (1.0 / D)
            cot = rb.at[1, line][clip * 32:clip * 32 + 32, :].astype(F32)
            gt = cot + inv[rows, 0:1] * (gn - mean_grad - nrm * mean_cross)
            rr.at[0, line][clip * 32:clip * 32 + 32, :] = gt.astype(BF)

        for k in (2, 1, 3):
            norm_back(m4(zl + k))
            back_copy(clip, k).start()
        norm_back(zl)
        rr.at[1, zl][clip * 32:clip * 32 + 32, :] = rr.at[0, zl][clip * 32:clip * 32 + 32, :]

    def back_copy(clip, k):
        part = pl.ds(clip * 32, 32)
        return copy(rr.at[0, m4(zl + k), part], rr.at[1, zl, part], c_s.at[clip, k], c_r.at[clip, k], at_zl(k))

    def e_copy(clip, k):
        return copy(rr2.at[0, clip, m4(x + k // 4) * 4 + m4(y + k % 4)], rr2.at[1, clip, xy],
                    e_s.at[clip, k], e_r.at[clip, k], at_xy(k))

    def line_row(o):
        return ((o >> 1) & 3) * 32 + (o >> 4) * 2 + (o & 1)

    both_halves = pick(lambda o: line_row(o) + ((o >> 3) & 1) * 128)
    top_half = pick(lambda o: jnp.where(((o >> 3) & 1) == 0, line_row(o), -1), 256, 128)

    def plane_start(clip):
        for k in (1, 2, 3):
            back_copy(clip, k).wait()
        block = rr[1, :, clip * 32:clip * 32 + 32, :].reshape(128, D)
        stacked = jnp.concatenate([block[:, 0:512], block[:, 640:1152]], axis=0)
        rr2[0, clip, :, :, 0:512] = dot(both_halves, stacked).astype(BF).reshape(16, 16, 512)
        rr2[0, clip, :, :, 512:640] = dot(top_half, block[:, 512:640]).astype(BF).reshape(16, 16, 128)

        for k in range(1, 16):
            e_copy(clip, k).start()

        rr2[1, clip, xy] = rr2[0, clip, xy]

    upper = pick(lambda o: (o >> 3) * 16 + (o & 7), 128, 256)
    lower = pick(lambda o: (o >> 3) * 16 + 8 + (o & 7), 128, 256)

    def finish(clip):
        for k in range(1, 16):
            e_copy(clip, k).wait()

        rows = rr2[1, clip].reshape(256, 640)
        out[clip, :, 0:640] = dot(upper, rows).astype(BF)
        out[clip, :, 640:1152] = dot(lower, rows[:, 0:512]).astype(BF)
        cp = pltpu.make_async_copy(out.at[clip], out_hbm.at[clip], out_sem.at[clip])
        cp.start()
        return cp

    places = (zl, x, y)

    def m_copy(step, k):
        to = (at_zl(k), dev(m4(x + k), y, zfull, c), dev(x, m4(y + k), zfull, c))[step]
        return copy(ms.at[step], mr.at[step, places[step]], m_s.at[step, k], m_r.at[step, k], to)

    def m_start(step):
        for k in (1, 2, 3):
            m_copy(step, k).start()
        mr[step, places[step]] = ms[step]

    def m_sum(step):
        for k in (1, 2, 3):
            m_copy(step, k).wait()
        return ((mr[step, 0] + mr[step, 1]) + mr[step, 2]) + mr[step, 3]

    attend(0)
    back_rows(0)
    attend(1)
    plane_start(0)
    back_rows(1)
    ms[1] = m_sum(0)
    m_start(1)
    stored_first = finish(0)
    ms[2] = m_sum(1)
    m_start(2)
    plane_start(1)
    total = m_sum(2)
    for clip in range(2):
        outm_ref[clip, :, 0:640] = total[2 * clip:2 * clip + 2]
        outm_ref[clip, :, 640:1152] = total[4 + 2 * clip:6 + 2 * clip, 0:512]
    stored_second = finish(1)
    stored_first.wait()
    stored_second.wait()


def local(tokens, modulation, cotangent, qkv_weight, out_weight):
    table = jnp.asarray(place_table(), BF)
    hbm = pl.BlockSpec(memory_space=pl.ANY)
    dma = pltpu.SemaphoreType.DMA
    vmem = pltpu.VMEM
    grad_tokens, grad_modulation = pl.pallas_call(
        kernel,
        out_shape=(
            jax.ShapeDtypeStruct((2, 128, D), BF),
            jax.ShapeDtypeStruct((2, 2, D), F32),
        ),
        in_specs=[hbm] * 6,
        out_specs=(hbm, pl.BlockSpec(memory_space=pltpu.VMEM)),
        scratch_shapes=[
            vmem((2, 2, 128, D), BF),
            vmem((3, 2, D), F32),
            vmem((18, 432), BF),
            vmem((18, 144), BF),
            vmem((2, 16, 16, D), BF),
            vmem((2, 16, 16, D), BF),
            vmem((2, 4, 64, D), BF),
            vmem((2, 4, 64, D), BF),
            vmem((2, 4, 4, 16, 768), BF),
            vmem((2, 4, 4, 80, D), BF),
            vmem((2, 4, 4, 64, D), BF),
            vmem((MAIN + 2 * TAIL, D), BF),
            vmem((256, D), BF),
            vmem((4, 2, 256, 256), BF),
            vmem((2, 256, TAIL), BF),
            vmem((256, D), BF),
            vmem((256, D), F32),
            vmem((256, 128), F32),
            vmem((4, 256, D), F32),
            vmem((4, 256, D), BF),
            vmem((3, 128, D), F32),
            vmem((3, 128, D), BF),
            vmem((128, MAIN + 2 * TAIL), BF),
            vmem((128, D), F32),
            vmem((2, 4, 64, D), BF),
            vmem((2, 2, 16, 16, 640), BF),
            vmem((2, 128, D), BF),
            vmem((3, 8, 640), F32),
            vmem((3, 4, 8, 640), F32),
            dma((6,)), dma((2,)),
            dma((4,)), dma((4,)), dma((3, 4)), dma((3, 4)), dma((4,)), dma((4,)),
            dma((2, 16)), dma((2, 16)), dma((2, 16)), dma((2, 16)),
            dma((2, 16)), dma((2, 16)), dma((2, 4)), dma((2, 4)),
            dma((2, 4)), dma((2, 4)), dma((2, 16)), dma((2, 16)),
            dma((3, 4)), dma((3, 4)),
        ],
        compiler_params=pltpu.CompilerParams(
            collective_id=0, has_side_effects=True, vmem_limit_bytes=60 * 1024 * 1024
        ),
        name="sublayer_backward",
    )(
        tokens.reshape(2, 128, D), modulation.transpose(1, 0, 2), cotangent.reshape(2, 128, D),
        qkv_weight, out_weight, table,
    )
    return grad_tokens.reshape(2, 1, 128, D), grad_modulation


def solution(mesh):
    in_specs = (
        P("dp", "seq", None, None),
        P("dp", None, None),
        P("dp", "seq", None, None),
        P("seq", "dp"),
        P("seq", "dp"),
    )
    out_specs = (P("dp", "seq", None, None), P("dp", None, None))
    return jax.shard_map(local, mesh=mesh, in_specs=in_specs, out_specs=out_specs, check_vma=False)
```

time: 124 us -> 114 us (0.919)
  Pallas kernels: 118 us -> 109 us
    pallas_call x1, Pallas kernels: 118 us -> 109 us  [local(): pl.pallas_call(kernel, out_shape=(jax.ShapeDtypeStruct((2, 128, D), BF),...]
    unnamed x0 -> x2, local copies, waits for them, and re-layouts: none -> 3.25 us
    reshape x2 -> x0, local copies, waits for them, and re-layouts: 2.55 us -> none  [the longest x1 1.92 us: local(): rows.reshape(16, 2, 8, D).transpose(1, 0, 2, 3).reshape(2, 1, 128, D)]
    slice x2 -> x0, local copies, waits for them, and re-layouts: 1.45 us -> none  [the longest x1 0.73 us: local(): sums[0:4, :]]
where the time goes in v3:
time: 114 us; the launch traced here: 113 us
  Pallas kernels  109 us (96%)
  local copies, waits for them, and re-layouts  3.25 us (3%)
    pallas_call x1, Pallas kernels, local(): pl.pallas_call(kernel, out_shape=(jax.ShapeDtypeStruct((2, 128, D), BF),...  109 us
    unnamed x2, local copies, waits for them, and re-layouts  3.25 us

profile of v3, /device:TPU:1, one launch (start us, length us, event | category | flops | bytes accessed | tf_op | source)
XLA Modules:
  0.0 112.7 jit_solution(10829167713936234790)
XLA Ops:
  0.6 108.8 %sublayer_backward.1 = (bf16[2,128,1152]{2,1,0:T(8,128)(2,1)}, f32[2,2,1152]{2,1,0:T(2,128)}) custom-call(bf16[2,128,1152]{2,1,0:T(8,128)(2,1)} %bitcast.7, f32[3,2,1152]{2,1,0:T(2,128)} %bitcast.9, bf16[2,128,1152]{2,1,0:T(8,128)(2,1)} %bitcast.8, bf16[18,432]{1,0:T(8,128)(2,1)} %wq_hbm.1, bf16[18,144]{1,0:T(8,128)(2,1)} %wo_hbm.1, ...), custom_call_target="tpu_custom_call" | custom-call | tf_op jit(solution)/shard_map/sublayer_backward/pallas_call | solution.py:559
  109.4 1.9 %copy.11 = bf16[2,1,128,1152]{3,2,1,0:T(8,128)(2,1)} copy(bf16[2,1,128,1152]{3,2,1,0:T(8,128)(2,1)} %bitcast.6) | data formatting | bytes 1179648
  111.4 1.3 %copy.12 = f32[2,2,1152]{2,1,0:T(2,128)} copy(f32[2,2,1152]{2,1,0:T(2,128)} %get-tuple-element.11) | data formatting | bytes 36864

commit v4 on v3

v4 whole, which is shorter than its diff:
```python
import functools
import math

import jax
import jax.numpy as jnp
import numpy as np
from jax import lax
from jax.experimental import pallas as pl
from jax.experimental.pallas import tpu as pltpu
from jax.sharding import PartitionSpec as P

D = 1152
H = 16
HD = 72
EPS = 1e-06
MESH = pl.DeviceIdType.MESH
BF = jnp.bfloat16
F32 = jnp.float32
RHS_T = (((1,), (1,)), ((), ()))
LHS_T = (((0,), (0,)), ((), ()))


MAIN, TAIL = 1024, 256


def place_table():
    table = np.zeros((MAIN + 2 * TAIL, D), np.float32)
    for feature in range(D):
        zl, rest = divmod(feature, 288)
        position, i = divmod(rest, 18)
        t = zl * 18 + i
        if t < 64:
            table[position * 64 + t, feature] = 1
        else:
            table[MAIN + position * 16 + t - 64, feature] = 1
            table[MAIN + TAIL + position * 16 + 8 + t - 64, feature] = 1
    return table


def dot(a, b, dims=(((1,), (0,)), ((), ()))):
    return lax.dot_general(a, b, dims, preferred_element_type=F32)


def iota(shape, dim):
    return lax.broadcasted_iota(jnp.int32, shape, dim)


def pick(source_row, n=256, m=256):
    return (source_row(iota((n, m), 0)) == iota((n, m), 1)).astype(F32).astype(BF)


def kernel(
    tok_hbm, mod_hbm, cot_hbm, wq_hbm, wo_hbm, table_hbm,
    out_hbm, outm_ref,
    raw, mod_ref, wq_ref, wo_ref,
    sa, ra, sb, rb, z, xs, xt, table, hid, hidg, hidt, gated, normed, inv, acc, acc_grad, pr, pr_grad, heads_acc, gp, gh_rows, gh, rr, rr2, out, ms, mr,
    in_sem, out_sem, zh_s, zh_r, zl_s, zl_r, w_s, w_r, wc_s, wc_r,
    a_s, a_r, b_s, b_r, c_s, c_r, e_s, e_r, m_s, m_r,
):
    s, q = lax.axis_index("seq"), lax.axis_index("dp")
    y, x, zl = lax.rem(s, 4), lax.rem(s // 4, 4), s // 16
    zh, c = q // 2, lax.rem(q, 2)
    xy = x * 4 + y
    zfull = zh * 4 + zl

    def m4(v):
        return lax.rem(v + 8, 4)

    def dev(x_, y_, z_, c_):
        return ((lax.rem(z_, 4) * 4 + x_) * 4 + y_, (z_ // 4) * 2 + c_)

    def at_xy(k):
        return dev(m4(x + k // 4), m4(y + lax.rem(k, 4)), zfull, c)

    def at_zl(k):
        return dev(x, y, zh * 4 + m4(zl + k), c)

    def at_zh(k):
        return dev(x, y, m4(zh + k) * 4 + zl, c)

    def at_ring(k):
        return dev(x, y, lax.rem(zfull + k + 16, 16), c)

    other = dev(x, y, zfull, 1 - c)

    def copy(src, dst, ss, rs, to):
        return pltpu.make_async_remote_copy(
            src_ref=src, dst_ref=dst, send_sem=ss, recv_sem=rs, device_id=to, device_id_type=MESH
        )

    loads = [
        pltpu.make_async_copy(src, dst, in_sem.at[n])
        for n, (src, dst) in enumerate((
            (wq_hbm, wq_ref), (wo_hbm, wo_ref), (tok_hbm, raw.at[0]), (cot_hbm, raw.at[1]),
            (mod_hbm, mod_ref), (table_hbm, table),
        ))
    ]
    for load in loads:
        load.start()

    barrier = pltpu.get_barrier_semaphore()

    def greet(to):
        pl.semaphore_signal(barrier, inc=1, device_id=to, device_id_type=MESH)

    for k in (1, 2, 3):
        greet(at_zh(k))
        greet(at_zl(k))
    for k in (1, -1, 2, -2):
        greet(at_ring(k))
    greet(other)

    @pl.loop(1, 16)
    def _(k):
        greet(at_xy(k))

    loads[0].wait()
    loads[1].wait()
    wide = jnp.concatenate(
        [wq_ref[...].astype(F32), wo_ref[...].astype(F32), jnp.zeros((18, 64), F32)], axis=1
    )
    ends = [wide[16 + j:17 + j, 128 * m:128 * m + 128] for j in range(2) for m in range(5)]
    ends = jnp.concatenate(ends + [jnp.zeros((6, 128), F32)], axis=0)
    z[zl, zh] = jnp.concatenate([wide[:16], ends], axis=1).astype(BF)

    to_plane = pick(lambda o: ((o >> 3) & 1) * 128 + (o >> 4) * 8 + (o & 7))

    def first_order(n):
        loads[2 + n].wait()
        sa[n] = dot(to_plane, raw[n].reshape(256, D)).astype(BF).reshape(16, 16, D)

    first_order(0)
    pl.semaphore_wait(barrier, 26)

    def zh_copy(k):
        ref = z.at[zl, zh]
        return copy(ref, ref, zh_s.at[k], zh_r.at[k], at_zh(k))

    ring = (1, -1, 2)

    def zl_copy(n, group):
        ref = z.at[zl, group]
        return copy(ref, ref, zl_s.at[n, group], zl_r.at[n, group], at_ring(ring[n]))

    def zl_arrived(n, group):
        ref = z.at[m4(zl - ring[n]), group]
        copy(ref, ref, zl_s.at[n, group], zl_r.at[n, group], at_ring(ring[n])).wait_recv()

    for k in (2, 1, 3):
        zh_copy(k).start()
    for n in range(3):
        zl_copy(n, zh).start()

    def a_copy(n, k):
        return copy(sa.at[n, m4(x + k // 4) * 4 + m4(y + lax.rem(k, 4))], ra.at[n, xy],
                    a_s.at[n, k], a_r.at[n, k], at_xy(k))

    def a_send(n):
        @pl.loop(1, 16)
        def _(k):
            a_copy(n, k).start()

        ra[n, xy] = sa[n, xy]

    a_send(0)
    first_order(1)
    a_send(1)

    for k in (1, 3, 2):
        zh_copy(k).wait_recv()
        for n in range(3):
            zl_copy(n, m4(zh - k)).start()

    def b_copy(n, k):
        return copy(sb.at[n, m4(zl + k)], rb.at[n, zl], b_s.at[n, k], b_r.at[n, k], at_zl(k))

    to_line = pick(lambda o: ((o >> 1) & 15) * 16 + ((o >> 5) & 1) * 8 + (o >> 6) * 2 + (o & 1))

    def second_step(n):
        @pl.loop(1, 16)
        def _(k):
            a_copy(n, k).wait()

        sb[n] = dot(to_line, ra[n].reshape(256, D)).astype(BF).reshape(4, 64, D)
        for k in (2, 1, 3):
            b_copy(n, k).start()
        rb[n, zl] = sb[n, zl]

    mine = zh // 2

    def rows_of(group):
        parts = []
        for k in range(4):
            stored = z[k, group].astype(F32)
            parts.append(stored[:, :640])
            for j in range(2):
                parts.append(jnp.concatenate(
                    [stored[5 * j + m:5 * j + m + 1, 640:768] for m in range(5)], axis=1
                ))
        return jnp.concatenate(parts, axis=0)

    def unit(half):
        for n in range(3):
            for b in range(2):
                zl_arrived(n, 2 * half + b)
        a, b = rows_of(2 * half), rows_of(2 * half + 1)
        return jnp.concatenate([a[:, :432], b[:, :432], a[:, 432:576], b[:, 432:576]], axis=1)

    first_axis = ((c, (1 - c)), ((1 - c), c))

    def shifted(st, i, j):
        fx, fy = first_axis[st]
        return m4(x + i * fx + j * fy), m4(y + i * fy + j * fx)

    def block_of(core, st, px, py):
        return xs.at[core, st, px, py, pl.ds(0, 64)] if st == 0 else xs.at[core, st, px, py]

    def held(st, i, j):
        px, py = shifted(st, i, j)
        return block_of(c, st, px, py)

    sent = []

    def w_send(st, i, j, to_i, to_j):
        ref = held(st, i, j)
        px, py = shifted(st, to_i, to_j)
        index = ((i - to_i) % 4) * 4 + (j - to_j) % 4
        cp = copy(ref, ref, w_s.at[st, index], w_r.at[st, index], dev(px, py, zfull, c))
        cp.start()
        sent.append(cp)

    def w_over(st, i, j):
        ref = held(st, i, j)
        index = i * 4 + j
        cp = copy(ref, ref, wc_s.at[st, index], wc_r.at[st, index], other)
        cp.start()
        sent.append(cp)

    def w_arrived(st, i, j):
        ref = held(st, i, j)
        index = i * 4 + j
        copy(ref, ref, w_s.at[st, index], w_r.at[st, index], other).wait_recv()
        w_over(st, i, j)

    def w_both_ways(st, i):
        w_send(st, i, 0, 0, 1)
        w_send(st, i, 0, 0, -1)

    def w_sides(st, i):
        w_arrived(st, i, 3)
        if i in (0, 2):
            w_send(st, i, 3, 0, 1)
        w_arrived(st, i, 1)
        if i in (1, 3):
            w_send(st, i, 1, 0, -1)

    def w_first(st):
        for i in (1, -1, 2):
            w_send(st, 0, 0, i, 0)
        w_both_ways(st, 0)
        w_over(st, 0, 0)

    second_step(0)
    near = unit(mine)
    xs[c, 0, x, y, 0:64, :] = near[:64].astype(BF)
    w_first(0)
    far = unit(1 - mine)
    xs[c, 1, x, y, 0:64, :] = far[:64].astype(BF)
    xs[c, 1, x, y, 64:80, :] = jnp.concatenate([
        jnp.where(mine == 0, near[64:], far[64:]), jnp.where(mine == 0, far[64:], near[64:])
    ], axis=0).astype(BF)
    w_first(1)
    second_step(1)
    for i in (1, 3):
        for st in range(2):
            w_arrived(st, i, 0)
            w_both_ways(st, i)
    for st in range(2):
        w_sides(st, 0)
    for st in range(2):
        w_arrived(st, 2, 0)
        w_both_ways(st, 2)

    def places_of(i):
        clip, lines = lax.rem(i, 2), pl.ds(pl.multiple_of(i // 2 * 2, 2), 2)
        rows = pl.ds(pl.multiple_of(clip * 128 + i // 2 * 64, 64), 64)
        return clip, lines, rows, pl.ds(pl.multiple_of(clip * 32, 32), 32)

    def norm_rows(i):
        clip, lines, rows, source = places_of(i)
        tile = rb[0, lines, source, :].reshape(64, D).astype(F32)
        mean = jnp.sum(tile, axis=1, keepdims=True) * (1.0 / D)
        centred = tile - mean
        inv_std = lax.rsqrt(jnp.sum(centred * centred, axis=1, keepdims=True) * (1.0 / D) + EPS)
        nrm = centred * inv_std
        normed[rows, :] = nrm
        inv[rows, :] = jnp.broadcast_to(inv_std, (64, 128))
        hid[rows, :] = (nrm * (1.0 + mod_ref[1, pl.ds(clip, 1), :]) + mod_ref[0, pl.ds(clip, 1), :]).astype(BF)

    def gate_rows(i):
        clip, lines, rows, source = places_of(i)
        cot = rb[1, lines, source, :].reshape(64, D).astype(F32)
        g = (cot * mod_ref[2, pl.ds(clip, 1), :]).astype(BF).astype(F32)
        for core in range(2):
            for half in range(2):
                d = 4 * half + core
                gated[core, half, rows, :] = jnp.concatenate([
                    jnp.zeros((64, 96), F32), g[:, 144 * d:144 * d + 144], g[:, 144 * d + 288:144 * d + 432]
                ], axis=1).astype(BF)

    def hidden_in(places):
        return dot(hid[...], places, RHS_T).astype(BF)

    def table_column(yj):
        return jnp.concatenate(
            [table[pl.ds(pl.multiple_of((k * 4 + yj) * 64, 64), 64), :] for k in range(4)], axis=0
        )

    def table_row(xj):
        return table[pl.ds(pl.multiple_of(xj * 256, 256), 256), :]

    def main_block(core, st, j, cols):
        if core != st:
            return xs[core, st, :, m4(y + j), 0:64, cols].reshape(256, -1)
        return xs[core, st, m4(x + j), :, 0:64, cols].reshape(256, -1)

    def tail_block(core, cols):
        return xs[core, 1, :, :, 64:80, cols].reshape(TAIL, -1)

    units = [(core, st) for core in range(2) for st in range(2)]

    def half_of(st):
        return lax.rem(mine + st, 2)

    def project(j, last=False):
        for core, st in units:
            for cols in (pl.ds(0, 512), pl.ds(512, 384)):
                now = dot(hidg[j, 0 if core != st else 1], main_block(core, st, j, cols))
                if j == 0:
                    acc[core, st, :, cols] = now
                elif not last:
                    acc[core, st, :, cols] += now
                else:
                    tail = dot(hidt[half_of(st)], tail_block(core, cols))
                    pr[core, half_of(st), :, cols] = (acc[core, st, :, cols] + now + tail).astype(BF)

    def by_columns_first(part):
        return jnp.concatenate([
            part[:, (b * 4 + a) * 64:(b * 4 + a) * 64 + 64] for a in range(4) for b in range(4)
        ], axis=1)

    def lanes_of(column, j):
        at = m4(y + j) if column else m4(x + j)
        return pl.ds(pl.multiple_of(at * 256, 256), 256)

    def upright_rows(j):
        for core, st in units:
            xt[core, st, :, lanes_of(core != st, j)] = main_block(core, st, j, pl.ds(0, 896)).T

    out_cols = pl.ds(768, 384)

    def project_grad(j):
        for column in (True, False):
            acc_grad[int(column), :, lanes_of(column, j)] = sum(
                dot(gated[core, half_of(st)], main_block(core, st, j, out_cols), RHS_T)
                for core, st in units if (core != st) == column
            )

    def place_grad():
        main = (acc_grad[0] + by_columns_first(acc_grad[1])).astype(BF)
        first, second = [
            sum(dot(gated[core, half], tail_block(core, out_cols), RHS_T) for core in range(2)) for half in range(2)
        ]
        ends = (first + pltpu.roll(second, TAIL - 8, 1)).astype(BF)
        pr_grad[...] = (dot(main, table[0:MAIN, :]) + dot(ends, table[MAIN:MAIN + TAIL, :])).astype(BF)

    def w_across(i, j):
        for st in range(2):
            px, py = shifted(1 - st, i, j)
            ref = block_of(1 - c, st, px, py)
            index = i * 4 + j
            copy(ref, ref, wc_s.at[st, index], wc_r.at[st, index], other).wait_recv()

    for k in (1, 2, 3):
        b_copy(0, k).wait()
    for load in loads[4:]:
        load.wait()
    pl.loop(0, 4)(norm_rows)
    for k in range(2):
        hidt[k] = hidden_in(table[MAIN + k * TAIL:MAIN + (k + 1) * TAIL, :])
    for j in range(4):
        hidg[j, 0] = hidden_in(table_column(m4(y + j)))
        hidg[j, 1] = hidden_in(table_row(m4(x + j)))
    for st in range(2):
        w_sides(st, 1)
    for i in range(4):
        w_across(i, 0)
    project(0)
    upright_rows(0)
    for i in (3, 2):
        for st in range(2):
            w_sides(st, i)
    for j in (3, 1):
        for i in range(4):
            w_across(i, j)
        project(j)
        upright_rows(j)
    for k in (1, 2, 3):
        b_copy(1, k).wait()
    pl.loop(0, 4)(gate_rows)
    for j in (0, 3, 1):
        project_grad(j)
    for i in range(4):
        for st in range(2):
            w_arrived(st, i, 2)
    for i in range(4):
        w_across(i, 2)
    project(2, last=True)
    project_grad(2)
    place_grad()
    upright_rows(2)
    for cp in sent:
        cp.wait_send()
    for k in (1, 2, 3):
        zh_copy(k).wait_send()
    for n in range(3):
        for k in range(4):
            zl_copy(n, m4(zh - k)).wait_send()

    score_scale = 1.0 / math.sqrt(HD)
    same = (iota((128, 256), 0) & 1) == (iota((128, 256), 1) & 1)

    def attend(clip):
        rows = pl.ds(clip * 128, 128)
        heads_acc[...] = jnp.zeros_like(heads_acc)

        def window_of(pair):
            d = pair // 3
            start = (3 * ((d // 2) % 2) + pair % 3) * 2 * HD
            return (d % 2, d // 4), pl.ds(start // 128 * 128, 256), start % 128

        def move(window, old, new):
            if old == new:
                return window
            return pltpu.roll(window.astype(F32), (new - old) % 256, 1).astype(BF)

        zero = jnp.zeros((128, 256), BF)
        lanes = iota((128, 256), 1)

        def by_head(window, offset):
            lane = lanes - offset
            return jnp.concatenate([
                jnp.where((lane >= 0) & (lane < HD), window, zero),
                jnp.where((lane >= HD) & (lane < 2 * HD), window, zero),
            ], axis=0)

        for i in range(H // 2):
            (qu, q_cols, q_at), (ku, k_cols, k_at), (vu, v_cols, v_at) = [window_of(n * 8 + i) for n in range(3)]
            g_at = i * 2 * HD % 128
            g_cols = pl.ds(i * 2 * HD // 128 * 128, 256)
            keys, values = pr[*ku, rows, k_cols], pr[*vu, rows, v_cols]
            queries = by_head(move(pr[*qu, rows, q_cols], q_at, k_at), k_at)
            grads = by_head(move(pr_grad[rows, g_cols], g_at, v_at), v_at)
            scores = dot(keys, queries, RHS_T) * score_scale
            e = jnp.exp(jnp.where(same, scores, -jnp.inf))
            probs = e * (1.0 / jnp.sum(e, axis=0, keepdims=True))
            grad_probs = dot(values, grads, RHS_T)
            inner = jnp.sum(probs * grad_probs, axis=0, keepdims=True)
            grad_scores = (probs * (grad_probs - inner) * score_scale).astype(BF)
            upright = jnp.concatenate([grad_scores[:, 0:128], grad_scores[:, 128:256]], axis=0)
            heads_acc[*qu, :, q_cols] += dot(upright, by_head(move(keys, k_at, q_at), q_at), LHS_T)
            heads_acc[*ku, :, k_cols] += dot(grad_scores, queries)
            heads_acc[*vu, :, v_cols] += dot(probs.astype(BF), grads)

        gp[...] = heads_acc[...].astype(BF)

    def back_rows(clip):
        by_row, by_column = [
            sum(dot(gp[core, half_of(st)], xt[core, st]) for core, st in units if (core != st) == column)
            for column in (False, True)
        ]
        gh_rows[:, 0:MAIN] = (by_row + by_columns_first(by_column)).astype(BF)
        tails = sum(
            dot(gp[core].reshape(256, 896), tail_block(core, pl.ds(0, 896)), RHS_T) for core in range(2)
        )
        gh_rows[:, MAIN:MAIN + TAIL] = tails[0:128].astype(BF)
        gh_rows[:, MAIN + TAIL:MAIN + 2 * TAIL] = tails[128:256].astype(BF)
        gh[...] = dot(gh_rows[...], table[...])

        shift_sum = jnp.sum(gh[...], axis=0, keepdims=True)
        scale_sum = jnp.sum(gh[...] * normed[clip * 128:clip * 128 + 128, :], axis=0, keepdims=True)
        for n, row in enumerate((shift_sum, scale_sum)):
            n += 2 * clip
            ms[0, n:n + 1, :] = row[:, 0:640]
            ms[0, n + 4:n + 5, 0:512] = row[:, 640:1152]
            ms[0, n + 4:n + 5, 512:640] = jnp.zeros((1, 128), F32)
        if clip == 1:
            m_start(0)

        for part in range(2):
            rows = pl.ds(clip * 128 + part * 64, 64)
            source = pl.ds(clip * 32, 32)
            grad_hidden = gh[part * 64:part * 64 + 64, :]
            nrm = normed[rows, :]
            gn = grad_hidden * (1.0 + mod_ref[1, clip:clip + 1, :])
            mean_grad = jnp.sum(gn, axis=1, keepdims=True) * (1.0 / D)
            mean_cross = jnp.sum(gn * nrm, axis=1, keepdims=True) * (1.0 / D)
            cot = rb[1, 2 * part:2 * part + 2, source, :].reshape(64, D).astype(F32)
            gt = cot + inv[rows, 0:1] * (gn - mean_grad - nrm * mean_cross)
            rr[0, 2 * part:2 * part + 2, source, :] = gt.astype(BF).reshape(2, 32, D)

        for piece in range(2):
            for k in (2, 1, 3):
                back_copy(clip, piece, k).start()
        rr.at[1, zl][clip * 32:clip * 32 + 32, :] = rr.at[0, zl][clip * 32:clip * 32 + 32, :]

    def back_copy(clip, piece, k):
        part = pl.ds(clip * 32 + piece * 16, 16)
        return copy(rr.at[0, m4(zl + k), part], rr.at[1, zl, part],
                    c_s.at[clip, piece, k], c_r.at[clip, piece, k], at_zl(k))

    def e_copy(clip, k):
        px, py = m4(x + k // 4), m4(y + lax.rem(k, 4))
        return copy(rr2.at[0, clip, px * 4 + py], rr2.at[1, clip, xy],
                    e_s.at[clip, k], e_r.at[clip, k], dev(px, py, zfull, c))

    def line_row(o):
        return ((o >> 1) & 3) * 16 + (o >> 4) * 2 + (o & 1)

    both_halves = pick(lambda o: line_row(o) + ((o >> 3) & 1) * 64, 128, 128)
    top_half = pick(lambda o: jnp.where(((o >> 3) & 1) == 0, line_row(o), -1), 128, 64)

    def plane_start(clip):
        for piece in range(2):
            for k in (1, 2, 3):
                back_copy(clip, piece, k).wait()
            source = pl.ds(clip * 32 + piece * 16, 16)
            to = pl.ds(piece * 8, 8)
            block = rr[1, :, source, :].reshape(64, D)
            stacked = jnp.concatenate([block[:, 0:512], block[:, 640:1152]], axis=0)
            rr2[0, clip, to, :, 0:512] = dot(both_halves, stacked).astype(BF).reshape(8, 16, 512)
            rr2[0, clip, to, :, 512:640] = dot(top_half, block[:, 512:640]).astype(BF).reshape(8, 16, 128)
            for a in range(2):
                i = m4(2 * piece + a - x)
                for j in (2, 1, 3):
                    e_copy(clip, i * 4 + j).start()

                @pl.when(i != 0)
                def _(i=i):
                    e_copy(clip, i * 4).start()

        rr2[1, clip, xy] = rr2[0, clip, xy]

    upper = pick(lambda o: (o >> 3) * 16 + (o & 7), 128, 256)
    lower = pick(lambda o: (o >> 3) * 16 + 8 + (o & 7), 128, 256)

    def finish(clip):
        for k in range(1, 16):
            e_copy(clip, k).wait()

        rows = rr2[1, clip].reshape(256, 640)
        out[clip, :, 0:640] = dot(upper, rows).astype(BF)
        out[clip, :, 640:1152] = dot(lower, rows[:, 0:512]).astype(BF)
        cp = pltpu.make_async_copy(out.at[clip], out_hbm.at[clip], out_sem.at[clip])
        cp.start()
        return cp

    places = (zl, x, y)

    def m_copy(step, k):
        to = (at_zl(k), dev(m4(x + k), y, zfull, c), dev(x, m4(y + k), zfull, c))[step]
        return copy(ms.at[step], mr.at[step, places[step]], m_s.at[step, k], m_r.at[step, k], to)

    def m_start(step):
        for k in (1, 2, 3):
            m_copy(step, k).start()
        mr[step, places[step]] = ms[step]

    def m_sum(step):
        for k in (1, 2, 3):
            m_copy(step, k).wait()
        return ((mr[step, 0] + mr[step, 1]) + mr[step, 2]) + mr[step, 3]

    attend(0)
    back_rows(0)
    attend(1)
    plane_start(0)
    back_rows(1)
    ms[1] = m_sum(0)
    m_start(1)
    stored_first = finish(0)
    ms[2] = m_sum(1)
    m_start(2)
    plane_start(1)
    total = m_sum(2)
    for clip in range(2):
        outm_ref[clip, :, 0:640] = total[2 * clip:2 * clip + 2]
        outm_ref[clip, :, 640:1152] = total[4 + 2 * clip:6 + 2 * clip, 0:512]
    stored_second = finish(1)
    stored_first.wait()
    stored_second.wait()


def local(tokens, modulation, cotangent, qkv_weight, out_weight):
    table = jnp.asarray(place_table(), BF)
    hbm = pl.BlockSpec(memory_space=pl.ANY)
    dma = pltpu.SemaphoreType.DMA
    vmem = pltpu.VMEM
    grad_tokens, grad_modulation = pl.pallas_call(
        kernel,
        out_shape=(
            jax.ShapeDtypeStruct((2, 128, D), BF),
            jax.ShapeDtypeStruct((2, 2, D), F32),
        ),
        in_specs=[hbm] * 6,
        out_specs=(hbm, pl.BlockSpec(memory_space=pltpu.VMEM)),
        scratch_shapes=[
            vmem((2, 2, 128, D), BF),
            vmem((3, 2, D), F32),
            vmem((18, 432), BF),
            vmem((18, 144), BF),
            vmem((2, 16, 16, D), BF),
            vmem((2, 16, 16, D), BF),
            vmem((2, 4, 64, D), BF),
            vmem((2, 4, 64, D), BF),
            vmem((4, 4, 16, 768), BF),
            vmem((2, 2, 4, 4, 80, D), BF),
            vmem((2, 2, 896, MAIN), BF),
            vmem((MAIN + 2 * TAIL, D), BF),
            vmem((256, D), BF),
            vmem((4, 2, 256, 256), BF),
            vmem((2, 256, TAIL), BF),
            vmem((2, 2, 256, 384), BF),
            vmem((256, D), F32),
            vmem((256, 128), F32),
            vmem((2, 2, 256, 896), F32),
            vmem((2, 256, MAIN), F32),
            vmem((2, 2, 256, 896), BF),
            vmem((256, D), BF),
            vmem((2, 2, 128, 896), F32),
            vmem((2, 2, 128, 896), BF),
            vmem((128, MAIN + 2 * TAIL), BF),
            vmem((128, D), F32),
            vmem((2, 4, 64, D), BF),
            vmem((2, 2, 16, 16, 640), BF),
            vmem((2, 128, D), BF),
            vmem((3, 8, 640), F32),
            vmem((3, 4, 8, 640), F32),
            dma((6,)), dma((2,)),
            dma((4,)), dma((4,)), dma((3, 4)), dma((3, 4)),
            dma((2, 16)), dma((2, 16)), dma((2, 16)), dma((2, 16)),
            dma((2, 16)), dma((2, 16)), dma((2, 4)), dma((2, 4)),
            dma((2, 2, 4)), dma((2, 2, 4)), dma((2, 16)), dma((2, 16)),
            dma((3, 4)), dma((3, 4)),
        ],
        compiler_params=pltpu.CompilerParams(
            collective_id=0, has_side_effects=True, vmem_limit_bytes=60 * 1024 * 1024
        ),
        name="sublayer_backward",
    )(
        tokens.reshape(2, 128, D), modulation.transpose(1, 0, 2), cotangent.reshape(2, 128, D),
        qkv_weight, out_weight, table,
    )
    return grad_tokens.reshape(2, 1, 128, D), grad_modulation


def solution(mesh):
    in_specs = (
        P("dp", "seq", None, None),
        P("dp", None, None),
        P("dp", "seq", None, None),
        P("seq", "dp"),
        P("seq", "dp"),
    )
    out_specs = (P("dp", "seq", None, None), P("dp", None, None))
    return jax.shard_map(local, mesh=mesh, in_specs=in_specs, out_specs=out_specs, check_vma=False)
```

time: 114 us -> 107 us (0.939)
  Pallas kernels: 109 us -> 103 us
    pallas_call x1, Pallas kernels: 109 us -> 103 us  [local(): pl.pallas_call(kernel, out_shape=(jax.ShapeDtypeStruct((2, 128, D), BF),...]
where the time goes in v4:
time: 107 us
  Pallas kernels  103 us (96%)
  local copies, waits for them, and re-layouts  3.25 us (3%)
    pallas_call x1, Pallas kernels, local(): pl.pallas_call(kernel, out_shape=(jax.ShapeDtypeStruct((2, 128, D), BF),...  103 us
    unnamed x2, local copies, waits for them, and re-layouts  3.25 us

profile of v4, /device:TPU:1, one launch (start us, length us, event | category | flops | bytes accessed | tf_op | source)
XLA Modules:
  0.0 106.6 jit_solution(1933413249715627066)
XLA Ops:
  0.6 102.7 %sublayer_backward.1 = (bf16[2,128,1152]{2,1,0:T(8,128)(2,1)}, f32[2,2,1152]{2,1,0:T(2,128)}) custom-call(bf16[2,128,1152]{2,1,0:T(8,128)(2,1)} %bitcast.7, f32[3,2,1152]{2,1,0:T(2,128)} %bitcast.9, bf16[2,128,1152]{2,1,0:T(8,128)(2,1)} %bitcast.8, bf16[18,432]{1,0:T(8,128)(2,1)} %wq_hbm.1, bf16[18,144]{1,0:T(8,128)(2,1)} %wo_hbm.1, ...), custom_call_target="tpu_custom_call" | custom-call | tf_op jit(solution)/shard_map/sublayer_backward/pallas_call | solution.py:609
  103.3 1.9 %copy.11 = bf16[2,1,128,1152]{3,2,1,0:T(8,128)(2,1)} copy(bf16[2,1,128,1152]{3,2,1,0:T(8,128)(2,1)} %bitcast.6) | data formatting | bytes 1179648
  105.2 1.3 %copy.12 = f32[2,2,1152]{2,1,0:T(2,128)} copy(f32[2,2,1152]{2,1,0:T(2,128)} %get-tuple-element.11) | data formatting | bytes 36864

commit v5 on v4

--- a/solution.py
+++ b/solution.py
@@ -110,8 +110,7 @@
         greet(at_ring(k))
     greet(other)
 
-    @pl.loop(1, 16)
-    def _(k):
+    for k in range(1, 16):
         greet(at_xy(k))
 
     loads[0].wait()
@@ -156,8 +155,7 @@
                     a_s.at[n, k], a_r.at[n, k], at_xy(k))
 
     def a_send(n):
-        @pl.loop(1, 16)
-        def _(k):
+        for k in (10, 8, 2, 9, 11, 6, 14, 5, 7, 13, 15, 4, 12, 1, 3):
             a_copy(n, k).start()
 
         ra[n, xy] = sa[n, xy]
@@ -177,8 +175,7 @@
     to_line = pick(lambda o: ((o >> 1) & 15) * 16 + ((o >> 5) & 1) * 8 + (o >> 6) * 2 + (o & 1))
 
     def second_step(n):
-        @pl.loop(1, 16)
-        def _(k):
+        for k in range(1, 16):
             a_copy(n, k).wait()
 
         sb[n] = dot(to_line, ra[n].reshape(256, D)).astype(BF).reshape(4, 64, D)
@@ -255,7 +252,7 @@
             w_send(st, i, 1, 0, -1)
 
     def w_first(st):
-        for i in (1, -1, 2):
+        for i in (1, -1):
             w_send(st, 0, 0, i, 0)
         w_both_ways(st, 0)
         w_over(st, 0, 0)
@@ -274,6 +271,8 @@
     for i in (1, 3):
         for st in range(2):
             w_arrived(st, i, 0)
+            if (st, i) in ((0, 3), (1, 1)):
+                w_send(st, i, 0, 1 if i == 3 else -1, 0)
             w_both_ways(st, i)
     for st in range(2):
         w_sides(st, 0)

time: 107 us -> 106 us (level)
  Pallas kernels: 103 us -> 101 us
    pallas_call x1, Pallas kernels: 103 us -> 101 us  [local(): pl.pallas_call(kernel, out_shape=(jax.ShapeDtypeStruct((2, 128, D), BF),...]
where the time goes in v5:
time: 106 us; the launch traced here: 105 us
  Pallas kernels  101 us (95%)
  local copies, waits for them, and re-layouts  3.25 us (3%)
    pallas_call x1, Pallas kernels, local(): pl.pallas_call(kernel, out_shape=(jax.ShapeDtypeStruct((2, 128, D), BF),...  101 us
    unnamed x2, local copies, waits for them, and re-layouts  3.25 us

profile of v5, /device:TPU:1, one launch (start us, length us, event | category | flops | bytes accessed | tf_op | source)
XLA Modules:
  0.0 105.3 jit_solution(9758467895738408704)
XLA Ops:
  0.6 101.4 %sublayer_backward.1 = (bf16[2,128,1152]{2,1,0:T(8,128)(2,1)}, f32[2,2,1152]{2,1,0:T(2,128)}) custom-call(bf16[2,128,1152]{2,1,0:T(8,128)(2,1)} %bitcast.7, f32[3,2,1152]{2,1,0:T(2,128)} %bitcast.9, bf16[2,128,1152]{2,1,0:T(8,128)(2,1)} %bitcast.8, bf16[18,432]{1,0:T(8,128)(2,1)} %wq_hbm.1, bf16[18,144]{1,0:T(8,128)(2,1)} %wo_hbm.1, ...), custom_call_target="tpu_custom_call" | custom-call | tf_op jit(solution)/shard_map/sublayer_backward/pallas_call | solution.py:608
  102.0 1.9 %copy.11 = bf16[2,1,128,1152]{3,2,1,0:T(8,128)(2,1)} copy(bf16[2,1,128,1152]{3,2,1,0:T(8,128)(2,1)} %bitcast.6) | data formatting | bytes 1179648
  103.9 1.3 %copy.12 = f32[2,2,1152]{2,1,0:T(2,128)} copy(f32[2,2,1152]{2,1,0:T(2,128)} %get-tuple-element.11) | data formatting | bytes 36864

commit v6 on v5

--- a/solution.py
+++ b/solution.py
@@ -172,6 +172,8 @@
     def b_copy(n, k):
         return copy(sb.at[n, m4(zl + k)], rb.at[n, zl], b_s.at[n, k], b_r.at[n, k], at_zl(k))
 
+    crossing = 3 - 2 * lax.rem(zl, 2)
+    line_order = (2, crossing, 4 - crossing)
     to_line = pick(lambda o: ((o >> 1) & 15) * 16 + ((o >> 5) & 1) * 8 + (o >> 6) * 2 + (o & 1))
 
     def second_step(n):
@@ -179,7 +181,7 @@
             a_copy(n, k).wait()
 
         sb[n] = dot(to_line, ra[n].reshape(256, D)).astype(BF).reshape(4, 64, D)
-        for k in (2, 1, 3):
+        for k in line_order:
             b_copy(n, k).start()
         rb[n, zl] = sb[n, zl]
 
@@ -509,7 +511,7 @@
             rr[0, 2 * part:2 * part + 2, source, :] = gt.astype(BF).reshape(2, 32, D)
 
         for piece in range(2):
-            for k in (2, 1, 3):
+            for k in line_order:
                 back_copy(clip, piece, k).start()
         rr.at[1, zl][clip * 32:clip * 32 + 32, :] = rr.at[0, zl][clip * 32:clip * 32 + 32, :]
 

time: 106 us -> 105 us (level)
    pallas_call x1, Pallas kernels: 101 us -> 100 us  [local(): pl.pallas_call(kernel, out_shape=(jax.ShapeDtypeStruct((2, 128, D), BF),...]
where the time goes in v6:
time: 105 us; the launch traced here: 104 us
  Pallas kernels  100 us (95%)
  local copies, waits for them, and re-layouts  3.25 us (3%)
    pallas_call x1, Pallas kernels, local(): pl.pallas_call(kernel, out_shape=(jax.ShapeDtypeStruct((2, 128, D), BF),...  100 us
    unnamed x2, local copies, waits for them, and re-layouts  3.25 us

profile of v6, /device:TPU:1, one launch (start us, length us, event | category | flops | bytes accessed | tf_op | source)
XLA Modules:
  0.0 104.0 jit_solution(4960943608379308853)
XLA Ops:
  0.6 100.1 %sublayer_backward.1 = (bf16[2,128,1152]{2,1,0:T(8,128)(2,1)}, f32[2,2,1152]{2,1,0:T(2,128)}) custom-call(bf16[2,128,1152]{2,1,0:T(8,128)(2,1)} %bitcast.7, f32[3,2,1152]{2,1,0:T(2,128)} %bitcast.9, bf16[2,128,1152]{2,1,0:T(8,128)(2,1)} %bitcast.8, bf16[18,432]{1,0:T(8,128)(2,1)} %wq_hbm.1, bf16[18,144]{1,0:T(8,128)(2,1)} %wo_hbm.1, ...), custom_call_target="tpu_custom_call" | custom-call | tf_op jit(solution)/shard_map/sublayer_backward/pallas_call | solution.py:610
  100.7 1.9 %copy.11 = bf16[2,1,128,1152]{3,2,1,0:T(8,128)(2,1)} copy(bf16[2,1,128,1152]{3,2,1,0:T(8,128)(2,1)} %bitcast.6) | data formatting | bytes 1179648
  102.7 1.3 %copy.12 = f32[2,2,1152]{2,1,0:T(2,128)} copy(f32[2,2,1152]{2,1,0:T(2,128)} %get-tuple-element.11) | data formatting | bytes 36864
